TPU v7x, 32 devices: a whole 2x2x4 slice. The times are simulated.
32 devices in a mesh: seq: 8 (over z, x), dp: 4 (over y, core).
Axes of the slice: x: 2, y: 2, z: 4, core: 2. Of those that a mesh axis runs over, the one named last changes fastest.
Arguments:
- tokens: bfloat16 [4, 4096, 4096], P('dp', 'seq'), may hold values from -6 to 6
- w_in: bfloat16 [4096, 2336], P(('seq', 'dp')), may hold values from -0.09375 to 0.09375
- conv_w: float32 [4, 2304], replicated, may hold values from -3 to 3
- a_rate: float32 [32], replicated, may hold values from 1.2207031e-05 to 0.06
- d_skip: float32 [32], replicated, may hold values from 0.5 to 2
- level_w: int32 [4, 11], P('dp'), may hold values from 0 to 256
- lengths: int32 [4], P('dp'), may hold values from 64 to 4096, as said below
Outputs:
- mixed_out: bfloat16 [4, 4096, 2048], P('dp', 'seq')
Inputs may be any that keep to these rules, and one draw needn't show every extreme that they name: `lengths`: every length is a multiple of 64, and some request has all 4096 positions live.
All inputs are finite; a program needn't handle non-finite values.
Results may differ from a plain program's by a relative error of at most 0.015.
Values may be sent and summed in bfloat16 or wider, within the bound.
A program may use at most 128 MiB of HBM per device.

v0:
```python
import jax
import jax.numpy as jnp
import numpy as np
from jax import lax
from jax.sharding import PartitionSpec as P

STATE = 128
Q = 64


def passed_along(array, axis, by):
    count = lax.axis_size(axis)
    pairs = [(i, i + by) for i in range(count) if 0 <= i + by < count]
    return lax.ppermute(array, axis, pairs)


def swapped(value, axis, stride):
    mask = 2**stride
    pairs = [(source, source ^ mask) for source in range(lax.axis_size(axis))]
    return lax.ppermute(value, axis, pairs)


def level_table(count):
    table = np.zeros((count, count), np.int32)
    for later in range(count):
        for earlier in range(later):
            table[later, earlier] = (earlier ^ later).bit_length()
    return table


def body(tokens, w_in, conv_w, a_rate, d_skip, level_w, lengths):
    token_rows = tokens.reshape(-1, tokens.shape[-1])
    count = token_rows.shape[0]
    projected = jnp.dot(
        token_rows,
        lax.all_gather(w_in, ("seq", "dp"), axis=0, tiled=True),
        preferred_element_type=jnp.float32,
    )
    kernel = conv_w.shape[0]
    channels = conv_w.shape[1]
    heads = a_rate.shape[0]
    inner = channels - 2 * STATE
    raw = projected[:, :channels].astype(jnp.bfloat16)
    rim = passed_along(raw[count - (kernel - 1) :], "seq", 1)
    padded = jnp.concatenate([rim, raw], 0)
    convolved = jnp.zeros((count, channels), jnp.float32)
    for offset in range(kernel):
        convolved = convolved + padded[offset : offset + count].astype(jnp.float32) * conv_w[offset]
    values = jax.nn.silu(convolved[:, :inner]).astype(jnp.bfloat16)
    in_b = convolved[:, inner : inner + STATE].astype(jnp.bfloat16)
    out_c = convolved[:, inner + STATE :].astype(jnp.bfloat16)
    step_size = jax.nn.softplus(projected[:, channels:])
    log_decay = -step_size * a_rate[None, :]
    head_dim = inner // heads
    driven = (
        values.astype(jnp.float32).reshape(count, heads, head_dim) * step_size[:, :, None]
    ).astype(jnp.bfloat16)
    stretches = count // Q
    cumul = jnp.cumsum(log_decay.reshape(stretches, Q, heads), axis=1)
    totals = cumul[:, -1]
    before = jnp.cumsum(totals, axis=0) - totals
    level_wt = level_w.reshape(-1).astype(jnp.float32) / 256.0
    keys_b = in_b.reshape(stretches, Q, STATE)
    query_c = out_c.reshape(stretches, Q, STATE)
    drive_c = driven.reshape(stretches, Q, heads, head_dim)
    scores = jnp.einsum("ctn,csn->cts", query_c, keys_b, preferred_element_type=jnp.float32)
    causal = jnp.asarray(np.tril(np.ones((Q, Q), bool)))[None, :, :, None]
    differ = cumul[:, :, None, :] - cumul[:, None, :, :]
    inner_wt = (
        jnp.where(causal, jnp.exp(jnp.where(causal, differ, 0.0)), 0.0)
        * scores[..., None]
        * level_wt[0]
    )
    inner_wt = inner_wt.astype(jnp.bfloat16)
    y_inner = jnp.einsum("ctsh,cshp->cthp", inner_wt, drive_c, preferred_element_type=jnp.float32)
    to_end = jnp.exp(totals[:, None, :] - cumul)
    weighted_b = (keys_b.astype(jnp.float32)[:, :, None, :] * to_end[..., None]).astype(
        jnp.bfloat16
    )
    states = jnp.einsum("cshn,cshp->chnp", weighted_b, drive_c, preferred_element_type=jnp.float32)
    local_bits = stretches.bit_length() - 1
    table = level_table(stretches)
    lower = jnp.asarray(np.tril(np.ones((stretches, stretches), bool), -1))[:, :, None]
    spacing = before[:, None, :] - before[None, :, :] - totals[None, :, :]
    mixing = (
        jnp.where(lower, jnp.exp(jnp.where(lower, spacing, 0.0)), 0.0) * level_wt[table][:, :, None]
    )
    carried = jnp.einsum("jih,ihnp->jhnp", mixing, states, precision=lax.Precision.HIGHEST)
    block_total = jnp.sum(totals, axis=0)
    to_block_end = jnp.exp(block_total[None, :] - before - totals)
    block_state = jnp.einsum("ih,ihnp->hnp", to_block_end, states, precision=lax.Precision.HIGHEST)
    position = lax.axis_index("seq")
    cross_state = jnp.zeros_like(block_state)
    passed = jnp.zeros_like(block_total)
    seq_bits = lax.axis_size("seq").bit_length() - 1
    for level in range(seq_bits):
        other_state, other_total = (
            swapped(block_state.astype(jnp.bfloat16), "seq", level).astype(block_state.dtype),
            swapped(block_total.astype(jnp.bfloat16), "seq", level).astype(block_total.dtype),
        )
        upper = (jnp.right_shift(position, level) & 1).astype(jnp.float32)
        cross_state = (
            cross_state
            + upper
            * level_wt[local_bits + level + 1]
            * jnp.exp(passed)[:, None, None]
            * other_state
        )
        passed = passed + upper * other_total
        block_state = jnp.where(
            upper > 0.5,
            other_state * jnp.exp(block_total)[:, None, None] + block_state,
            block_state * jnp.exp(other_total)[:, None, None] + other_state,
        )
        block_total = block_total + other_total
    carried = carried + jnp.exp(before)[:, :, None, None] * cross_state[None]
    carried_low = carried.astype(jnp.bfloat16)
    y_cross = jnp.exp(cumul)[..., None] * jnp.einsum(
        "ctn,chnp->cthp", query_c, carried_low, preferred_element_type=jnp.float32
    )
    output = (
        y_inner
        + y_cross
        + d_skip[None, None, :, None]
        * values.astype(jnp.float32).reshape(stretches, Q, heads, head_dim)
    )
    output = output * lax.rsqrt(jnp.mean(output * output, axis=-1, keepdims=True) + 1e-05)
    places = (position * count + jnp.arange(count, dtype=jnp.int32)).reshape(stretches, Q)
    output = jnp.where((places < lengths[0])[:, :, None, None], output, 0.0)
    return output.reshape(1, count, inner).astype(jnp.bfloat16)


def solution(mesh):
    in_specs = (P("dp", "seq", None), P(("seq", "dp"), None), P(), P(), P(), P("dp", None), P("dp"))
    out_specs = P("dp", "seq", None)
    return jax.shard_map(body, mesh=mesh, in_specs=in_specs, out_specs=out_specs, check_vma=False)
```

profile of v0, /device:TPU:24, one launch (start us, length us, event | category | flops | bytes accessed | tf_op | source)
XLA Modules:
  0.0 311.9 jit_solution(9234794315503434707)
XLA Ops:
  6.5 0.7 all-gather.2.cloned.1.call-update
  7.3 1.6 slice_reduce_fusion.3
  8.9 1.2 fusion.48
  10.1 126.0 %all-gather.2.cloned.1.call-done = bf16[4096,2336]{0,1:T(8,128)(2,1)} async-done(((bf16[128,2336]{0,1:T(8,128)(2,1)}), bf16[4096,2336]{0,1:T(8,128)(2,1)}) %all-gather.2.cloned.1.call-update) | async-done | bytes 19136528 | tf_op jit(solution)/shard_map/all_gather | solution.py:36
  136.1 14.7 %fusion.57 = (bf16[512,2336]{0,1:T(8,128)(2,1)S(1)}, f32[512,2336]{0,1:T(8,128)S(1)}) fusion(bf16[4096,2336]{0,1:T(8,128)(2,1)} %all-gather.2.cloned.1.call-done, bf16[1,512,4096]{2,1,0:T(8,128)(2,1)} %param.11), kind=kOutput, calls=%fused_computation.95 | convolution fusion | flops 9799090176 | bytes 30507008 | tf_op jit(solution)/shard_map/dot_general | solution.py:34
  150.8 0.8 compare_select_fusion
  151.6 0.1 reshape.121
  151.7 0.2 copy.37
  151.8 6.3 %fusion.58 = f32[8,64,32]{2,0,1:T(8,128)S(1)} fusion(f32[8,64,32]{2,0,1:T(8,128)S(1)} %copy.37), kind=kOutput, calls=%fused_computation.97 | output fusion | flops 1032192 | bytes 131072 | tf_op jit(solution)/shard_map/jit(cumsum)/reduce_window_sum | solution.py:59
  158.2 1.1 fusion.43
  159.3 0.6 fusion.51
  159.9 0.8 fusion.55
  160.7 0.2 slice.82
  160.9 0.9 copy.33
  161.8 3.3 %collective-permute-start = (bf16[3,2304]{1,0:T(4,128)(2,1)}, bf16[3,2304]{1,0:T(4,128)(2,1)}, u32[]{:S(2)}, u32[]{:S(2)}) collective-permute-start(bf16[3,2304]{1,0:T(4,128)(2,1)} %copy.33), channel_id=1, source_target_pairs={{0,4},{4,8},{8,12},{12,16},{16,20},{20,24},{24,28},{1,5},{5,9},{9,... | collective-permute-start | bytes 41480 | tf_op jit(solution)/shard_map/ppermute | solution.py:14
  165.1 0.7 exponential_bitcast_fusion
  165.8 1.8 slice.83
  167.7 0.8 copy.43
  168.5 0.1 mul.241
  168.6 0.7 copy.35
  169.2 0.0 collective-permute-done
  169.2 1.1 copy.34
  170.4 5.9 %fusion.53 = (bf16[512,2304]{0,1:T(8,128)(2,1)S(1)}, f32[512,2304]{0,1:T(8,128)}) fusion(f32[2304]{0:T(1024)S(1)} %get-tuple-element.7, bf16[512,2304]{0,1:T(8,128)(2,1)S(1)} %slice.83, f32[2304]{0:T(1024)S(1)} %copy-done.5, bf16[3,2304]{0,1:T(8,128)(2,1)S(1)} %copy.34, f32[2304]{0:T(1024)S(1)} %get-tuple-element.6, f32[2304]{0:T(1024)S(1)} %get-tuple-element.5), kind=kLoop, calls=%fused_computation.91 | loop fusion | flops 24772608 | bytes 9487872 | tf_op jit(solution)/shard_map/convert.2
  176.3 0.1 copy.41
  176.4 5.2 %fusion.18 = f32[512,2048]{0,1:T(8,128)} fusion(f32[512,2304]{0,1:T(8,128)} %get-tuple-element.12), kind=kLoop, calls=%fused_computation.34 | loop fusion | flops 6291456 | bytes 8388608 | tf_op jit(solution)/shard_map/reshape | solution.py:56
  181.7 7.1 %reshape.125 = f32[8,64,32,64]{1,0,3,2:T(8,128)} reshape(f32[512,2048]{0,1:T(8,128)} %fusion.18) | data formatting | bytes 8388608 | tf_op jit(solution)/shard_map/reshape | solution.py:56
  188.8 9.9 %multiply_reduce_fusion = (f32[32,128,64]{1,2,0:T(8,128)S(1)}, f32[8,32,128,64]{2,3,1,0:T(8,128)}) fusion(f32[32,8]{0,1:T(8,128)S(1)} %exponential_bitcast_fusion, f32[8,64,32]{1,2,0:T(8,128)S(1)} %copy-done.2, f32[8,64,128]{2,1,0:T(8,128)S(1)} %bitcast_convert_fusion, f32[8,64,32,64]{1,0,3,2:T(8,128)} %reshape.125, f32[8,64,32]{1,2,0:T(8,128)S(1)} %copy-done.3), kind=kOutput, calls=%fused_computation.5 | convolution fusion | flops 278659072 | bytes 14025728 | tf_op jit(solution)/shard_map/cshn,cshp->chnp/dot_general | solution.py:80
  198.8 0.1 convert_element_type.108
  198.9 0.1 collective-permute-start.1
  199.0 0.6 fusion.56
  200.3 2.1 collective-permute-start.2
  202.4 10.4 %collective-permute-done.2 = bf16[32]{0:T(256)(128)(2,1)S(1)} collective-permute-done((bf16[32]{0:T(256)(128)(2,1)S(1)}, bf16[32]{0:T(256)(128)(2,1)S(1)}, u32[]{:S(2)}, u32[]{:S(2)}) %collective-permute-start.2) | collective-permute-done | bytes 96 | tf_op jit(solution)/shard_map/ppermute | solution.py:20
  212.8 1.6 collective-permute-start.4
  215.1 1.4 collective-permute-done.4
  216.4 0.0 collective-permute-done.1
  216.4 1.1 fusion.50
  217.6 1.5 collective-permute-start.3
  219.1 10.4 %collective-permute-done.3 = bf16[32,128,64]{1,2,0:T(8,128)(2,1)S(1)} collective-permute-done((bf16[32,128,64]{1,2,0:T(8,128)(2,1)}, bf16[32,128,64]{1,2,0:T(8,128)(2,1)S(1)}, u32[]{:S(2)}, u32[]{:S(2)}) %collective-permute-start.3) | collective-permute-done | bytes 524320 | tf_op jit(solution)/shard_map/ppermute | solution.py:20
  229.5 2.1 fusion.25
  231.6 3.0 collective-permute-start.5
  235.2 0.8 gather_fusion
  236.0 0.1 reshape.127
  236.8 0.1 copy.45
  236.9 0.1 copy.46
  236.9 0.1 copy.38
  237.1 0.1 copy.48
  237.1 0.1 copy.44
  237.2 0.1 copy.42
  237.4 0.1 copy.40
  237.5 0.2 fusion.59
  237.7 17.4 %collective-permute-done.5 = bf16[32,128,64]{1,2,0:T(8,128)(2,1)S(1)} collective-permute-done((bf16[32,128,64]{1,2,0:T(8,128)(2,1)}, bf16[32,128,64]{1,2,0:T(8,128)(2,1)S(1)}, u32[]{:S(2)}, u32[]{:S(2)}) %collective-permute-start.5) | collective-permute-done | bytes 524320 | tf_op jit(solution)/shard_map/ppermute | solution.py:20
  255.1 0.3 fusion.20
  255.5 16.3 %fusion = bf16[8,32,128,64]{2,0,3,1:T(8,128)(2,1)S(1)} fusion(f32[32,128,64]{1,2,0:T(8,128)S(1)} %fusion.20, f32[8,32]{0,1:T(8,128)S(1)} %copy.48, f32[8,32,128,64]{2,3,1,0:T(8,128)} %get-tuple-element.37, f32[8,8]{1,0:T(8,128)S(1)} %reshape.127, f32[8,32]{0,1:T(8,128)S(1)} %copy.46, f32[8,32]{0,1:T(8,128)S(1)} %copy.45, f32[8,32]{0,1:T(8,128)S(1)} %copy.44, ...), kind=kOutput, calls=%fused_computation.2 | convolution fusion | flops 207628288 | bytes 13635904 | tf_op jit(solution)/shard_map/jih,ihnp->jhnp/dot_general | solution.py:88
  271.7 0.0 slice-start
  271.7 1.1 copy.49
  272.9 0.0 slice-start.1
  272.9 0.0 copy-start.14
  272.9 0.0 copy-start.15
  272.9 1.2 fusion.60
  274.1 1.3 slice-done.1
  275.4 8.8 %multiply_reduce_fusion.1 = (f32[8,64,32]{1,2,0:T(8,128)S(1)}, f32[8,64,32,64]{1,3,2,0:T(8,128)}) fusion(f32[8,64,32,64]{1,0,3,2:T(8,128)S(1)} %bitcast.68, f32[32]{0:T(128)S(1)} %copy-done.14, f32[8,64,32,64]{1,3,2,0:T(8,128)S(1)} %bitcast.70, f32[8,64,32]{1,2,0:T(8,128)S(1)} %copy.42, f32[]{:T(128)} %bitcast.6, f32[8,64,64]{2,1,0:T(8,128)S(1)} %fusion.59, ...), kind=kOutput, calls=%fused_computation.9 | convolution fusion | flops 148881408 | bytes 12980356 | tf_op jit(solution)/shard_map/ctsh,cshp->cthp/dot_general | solution.py:75
  284.2 7.0 %select_convert_fusion = bf16[8,64,32,64]{1,3,2,0:T(8,128)(2,1)} fusion(f32[8,64,32,64]{1,3,2,0:T(8,128)} %get-tuple-element.39, f32[8,64,32]{1,2,0:T(8,128)S(1)} %add_rsqrt_fusion, pred[8,64]{1,0:T(8,128)(4,1)S(1)} %add_compare_fusion), kind=kLoop, calls=%fused_computation.8 | loop fusion | flops 3145728 | bytes 6357504 | tf_op jit(solution)/shard_map/convert_element_type | solution.py:130
  291.2 7.1 %copy.51 = bf16[8,64,32,64]{3,2,1,0:T(8,128)(2,1)} copy(bf16[8,64,32,64]{1,3,2,0:T(8,128)(2,1)} %select_convert_fusion) | data formatting | bytes 4194304 | tf_op jit(solution)/shard_map/convert_element_type | solution.py:130
  298.3 6.7 %convert_element_type.122 = bf16[1,512,2048]{2,1,0:T(8,128)(2,1)} reshape(bf16[8,64,32,64]{3,2,1,0:T(8,128)(2,1)} %copy.51) | data formatting | bytes 4194304 | tf_op jit(solution)/shard_map/convert_element_type | solution.py:130
  (43 shorter events, 0.2 us)
Async XLA Ops:
  6.5 129.6 %all-gather.2.cloned.1.call-start = ((), (), s32[]{:S(2)}) async-start(), calls=%async_computation | async-start | bytes 19734528 | tf_op jit(solution)/shard_map/all_gather | solution.py:36
  10.1 140.7 %copy-start.12 = (f32[32]{0:T(128)S(1)}, f32[32]{0:T(128)}, u32[]{:S(2)}) copy-start(f32[32]{0:T(128)} %param.14) | copy-start | bytes 388
  150.8 14.3 %copy-start = (bf16[512,2336]{0,1:T(8,128)(2,1)}, bf16[512,2336]{0,1:T(8,128)(2,1)S(1)}, u32[]{:S(2)}) copy-start(bf16[512,2336]{0,1:T(8,128)(2,1)S(1)} %get-tuple-element.34) | copy-start | bytes 7176196
  161.8 5.9 %copy-start.1 = (f32[8,64,32]{2,0,1:T(8,128)S(1)}, f32[8,64,32]{2,0,1:T(8,128)}, u32[]{:S(2)}) copy-start(f32[8,64,32]{2,0,1:T(8,128)} %get-tuple-element.18) | copy-start | bytes 196612
  161.8 6.7 %copy-start.4 = (f32[512,32]{0,1:T(8,128)S(1)}, f32[512,32]{0,1:T(8,128)}, u32[]{:S(2)}) copy-start(f32[512,32]{0,1:T(8,128)} %get-tuple-element.13) | copy-start | bytes 196612
  161.8 7.5 %collective-permute-start = (bf16[3,2304]{1,0:T(4,128)(2,1)}, bf16[3,2304]{1,0:T(4,128)(2,1)}, u32[]{:S(2)}, u32[]{:S(2)}) collective-permute-start(bf16[3,2304]{1,0:T(4,128)(2,1)} %copy.33), channel_id=1, source_target_pairs={{0,4},{4,8},{8,12},{12,16},{16,20},{20,24},{24,28},{1,5},{5,9},{9,... | collective-permute-start | bytes 41480 | tf_op jit(solution)/shard_map/ppermute | solution.py:14
  165.8 4.5 %copy-start.5 = (f32[2304]{0:T(1024)S(1)}, f32[2304]{0:T(1024)}, u32[]{:S(2)}) copy-start(f32[2304]{0:T(1024)} %get-tuple-element.8) | copy-start | bytes 27652
  181.7 7.1 %copy-start.2 = (f32[8,64,32]{1,2,0:T(8,128)S(1)}, f32[8,64,32]{1,2,0:T(8,128)}, u32[]{:S(2)}) copy-start(f32[8,64,32]{1,2,0:T(8,128)} %copy.43) | copy-start | bytes 196612
  181.7 7.1 %copy-start.3 = (f32[8,64,32]{1,2,0:T(8,128)S(1)}, f32[8,64,32]{1,2,0:T(8,128)}, u32[]{:S(2)}) copy-start(f32[8,64,32]{1,2,0:T(8,128)} %copy.35) | copy-start | bytes 196612
  188.8 10.1 %copy-start.9 = (f32[1,11]{1,0:T(1,128)S(1)}, f32[1,11]{1,0:T(1,128)}, u32[]{:S(2)}) copy-start(f32[1,11]{1,0:T(1,128)} %get-tuple-element.28) | copy-start | bytes 136
  188.8 11.4 %copy-start.10 = (f32[32]{0:T(128)S(1)}, f32[32]{0:T(128)}, u32[]{:S(2)}) copy-start(f32[32]{0:T(128)} %get-tuple-element.20) | copy-start | bytes 388
  198.8 36.5 %copy-start.13 = (s32[64]{0:T(128)S(1)}, s32[64]{0:T(128)}, u32[]{:S(2)}) copy-start(s32[64]{0:T(128)} %constant.57) | copy-start | bytes 772
  198.8 37.9 %copy-start.6 = (f32[8,32]{1,0:T(8,128)S(1)}, f32[8,32]{1,0:T(8,128)}, u32[]{:S(2)}) copy-start(f32[8,32]{1,0:T(8,128)} %get-tuple-element.10) | copy-start | bytes 3076
  198.9 38.2 %copy-start.8 = (f32[8,32]{1,0:T(8,128)S(1)}, f32[8,32]{1,0:T(8,128)}, u32[]{:S(2)}) copy-start(f32[8,32]{1,0:T(8,128)} %get-tuple-element.9) | copy-start | bytes 3076
  198.9 17.6 %collective-permute-start.1 = (bf16[32,128,64]{1,2,0:T(8,128)(2,1)S(1)}, bf16[32,128,64]{1,2,0:T(8,128)(2,1)S(1)}, u32[]{:S(2)}, u32[]{:S(2)}) collective-permute-start(bf16[32,128,64]{1,2,0:T(8,128)(2,1)S(1)} %convert_element_type.108), channel_id=1, source_target_pairs={{0,4},{4,0},{8,12},{12,8},{16,20},{20,16},{24,28},{28,24},{1,5},{5... | collective-permute-start | bytes 1572872 | tf_op jit(solution)/shard_map/ppermute | solution.py:20
  200.3 36.9 %copy-start.7 = (f32[8,32]{1,0:T(8,128)S(1)}, f32[8,32]{1,0:T(8,128)}, u32[]{:S(2)}) copy-start(f32[8,32]{1,0:T(8,128)} %get-tuple-element.19) | copy-start | bytes 3076
  200.3 12.5 %collective-permute-start.2 = (bf16[32]{0:T(256)(128)(2,1)S(1)}, bf16[32]{0:T(256)(128)(2,1)S(1)}, u32[]{:S(2)}, u32[]{:S(2)}) collective-permute-start(bf16[32]{0:T(256)(128)(2,1)S(1)} %convert_element_type.111), channel_id=1, source_target_pairs={{0,4},{4,0},{8,12},{12,8},{16,20},{20,16},{24,28},{28,24},{1,5},{5... | collective-permute-start | bytes 200 | tf_op jit(solution)/shard_map/ppermute | solution.py:20
  212.8 3.6 %collective-permute-start.4 = (bf16[32]{0:T(256)(128)(2,1)S(1)}, bf16[32]{0:T(256)(128)(2,1)S(1)}, u32[]{:S(2)}, u32[]{:S(2)}) collective-permute-start(bf16[32]{0:T(256)(128)(2,1)S(1)} %get-tuple-element.22), channel_id=1, source_target_pairs={{0,8},{4,12},{8,0},{12,4},{16,24},{20,28},{24,16},{28,20},{1,9},{5... | collective-permute-start | bytes 200 | tf_op jit(solution)/shard_map/ppermute | solution.py:20
  217.6 12.0 %collective-permute-start.3 = (bf16[32,128,64]{1,2,0:T(8,128)(2,1)}, bf16[32,128,64]{1,2,0:T(8,128)(2,1)S(1)}, u32[]{:S(2)}, u32[]{:S(2)}) collective-permute-start(bf16[32,128,64]{1,2,0:T(8,128)(2,1)} %fusion.50), channel_id=1, source_target_pairs={{0,8},{4,12},{8,0},{12,4},{16,24},{20,28},{24,16},{28,20},{1,9},{5... | collective-permute-start | bytes 1572872 | tf_op jit(solution)/shard_map/ppermute | solution.py:20
  231.6 23.8 %copy-start.11 = (pred[8,8]{1,0:T(8,128)(4,1)S(1)}, pred[8,8]{1,0:T(8,128)(4,1)}, u32[]{:S(2)}) copy-start(pred[8,8]{1,0:T(8,128)(4,1)} %constant.50.clone) | copy-start | bytes 196
  231.6 23.5 %collective-permute-start.5 = (bf16[32,128,64]{1,2,0:T(8,128)(2,1)}, bf16[32,128,64]{1,2,0:T(8,128)(2,1)S(1)}, u32[]{:S(2)}, u32[]{:S(2)}) collective-permute-start(bf16[32,128,64]{1,2,0:T(8,128)(2,1)} %fusion.25), channel_id=1, source_target_pairs={{0,16},{4,20},{8,24},{12,28},{16,0},{20,4},{24,8},{28,12},{1,17},{... | collective-permute-start | bytes 1572872 | tf_op jit(solution)/shard_map/ppermute | solution.py:20
  271.7 2.4 slice-start
  272.9 2.6 slice-start.1
  272.9 2.6 copy-start.14
  272.9 2.5 copy-start.15
Sparse Core Ops, SparseCore 0:
  8.9 127.1 all-gather.1
where the time goes:
time: 316 us; the launch traced here: 312 us
  waiting for transfers between devices  166 us (53%)
  matrix products  51.1 us (16%)
  local copies, waits for them, and re-layouts  33.3 us (11%)
  other arithmetic  33.3 us (11%)
  between operations  16.3 us (5%)
  starting transfers between devices  11.6 us (4%)
    all_gather x1, waiting for transfers between devices, body(): lax.all_gather(w_in, ('seq', 'dp'), axis=0, tiled=True)  126 us
    ppermute x5, waiting for transfers between devices, swapped(): return lax.ppermute(value, axis, pairs)  39.6 us
    dot_general x1, matrix products, body(): jnp.einsum('jih,ihnp->jhnp', mixing, states, precision=lax.Precision.HIGH...  16.3 us
    dot_general x1, matrix products, body(): jnp.dot(token_rows, lax.all_gather(w_in, ('seq', 'dp'), axis=0, tiled=Tru...  14.7 us
    convert_element_type x2, local copies, waits for them, and re-layouts, body(): return output.reshape(1, count, inner).astype(jnp.bfloat16)  13.9 us
    dot_general x1, matrix products, body(): jnp.einsum('cshn,cshp->chnp', weighted_b, drive_c, preferred_element_type...  9.94 us
    dot_general x1, matrix products, body(): jnp.einsum('ctsh,cshp->cthp', inner_wt, drive_c, preferred_element_type=j...  8.76 us
    ppermute x5, starting transfers between devices, swapped(): return lax.ppermute(value, axis, pairs)  8.26 us
  transfers between devices with their start and end apart: 7, of which 5 were waited for; matrix products, arithmetic and copies ran while one was open for 3% of the time, Pallas kernels for 0%

commit v1 on v0

v1 whole, which is shorter than its diff:
```python
import functools

import jax
import jax.numpy as jnp
from jax import lax
from jax.experimental import pallas as pl
from jax.experimental.pallas import tpu as pltpu
from jax.sharding import PartitionSpec as P

STATE = 128
Q = 64
RIM = 16
LANES = 128
WIDE = 512
HEAD = 64
MESH = pl.DeviceIdType.MESH
F32 = jnp.float32
BF16 = jnp.bfloat16


def dot(a, b):
    return jnp.dot(a, b, preferred_element_type=F32)


def chunk_list(inner, padded):
    chunks = [(inner, padded - inner)]
    chunks += [(at, WIDE) for at in range(0, inner, WIDE)]
    return chunks


def project_kernel(
    nz, n, inner, tok_ref, w_ref, raw_ref, step_ref, ext, wbuf, tok_sem, rim_sem, own_sem, send_sem, recv_sem, core_send, core_recv
):
    seq = lax.axis_index("seq")
    dp = lax.axis_index("dp")
    nseq = nz * n
    z, x = seq // n, seq % n
    y, core = dp // 2, dp % 2
    rows = w_ref.shape[0]
    count = tok_ref.shape[0]
    padded = w_ref.shape[1]
    chunks = chunk_list(inner, padded)
    after = (seq + 1) % nseq
    prior = (seq + nseq - 1) % nseq

    def place(dz, da, db):
        dx = da * (1 - core) + db * core
        dy = da * core + db * (1 - core)
        return ((z + dz) % nz) * n + (x + dx) % n, ((y + dy) % n) * 2 + core

    def rows_of(device):
        at = device[0] * (2 * n) + device[1]
        return pl.ds(pl.multiple_of(at * rows, rows), rows)

    offsets = [(dz, da, db) for dz in range(nz) for da in range(n) for db in range(n)]
    peers = [(dz, 0, 0) for dz in range(1, nz)]
    peers += [(0, da, 0) for da in range(1, n)] + [(0, 0, db) for db in range(1, n)]
    other = (seq, y * 2 + 1 - core)

    barrier = pltpu.get_barrier_semaphore()
    greeted = [place(*peer) for peer in peers] + [other, (after, dp), (prior, dp)]
    for device in greeted:
        pl.semaphore_signal(barrier, inc=1, device_id=device, device_id_type=MESH)
    pl.semaphore_wait(barrier, len(greeted))

    rim = pltpu.make_async_remote_copy(
        src_ref=tok_ref.at[pl.ds(count - RIM, RIM)],
        dst_ref=ext.at[pl.ds(0, RIM)],
        send_sem=rim_sem.at[0],
        recv_sem=rim_sem.at[1],
        device_id=(after, dp),
        device_id_type=MESH,
    )
    own_rows = rows_of((seq, dp))
    number = {offset: at for at, offset in enumerate(offsets)}
    sends = []

    def link_copy(c, offset, step):
        at, width = chunks[c]
        cols = pl.ds(at, width)
        where = rows_of(place(*offset))
        mine = offset == (0, 0, 0)
        lands = tuple((o - s) % m for o, s, m in zip(offset, step, (nz, n, n)))
        slot = number[lands]
        return pltpu.make_async_remote_copy(
            src_ref=w_ref.at[:, cols] if mine else wbuf.at[where, cols],
            dst_ref=wbuf.at[where, cols],
            send_sem=send_sem.at[c, slot],
            recv_sem=recv_sem.at[c, slot],
            device_id=place(*step),
            device_id_type=MESH,
        )

    def arrived(c, offset):
        at, width = chunks[c]
        ref = wbuf.at[rows_of(place(*offset)), pl.ds(at, width)]
        pltpu.make_async_copy(ref, ref, recv_sem.at[c, number[offset]]).wait()

    def core_copy(c, offset):
        at, width = chunks[c]
        cols = pl.ds(at, width)
        where = rows_of(place(*offset))
        mine = offset == (0, 0, 0)
        return pltpu.make_async_remote_copy(
            src_ref=w_ref.at[:, cols] if mine else wbuf.at[where, cols],
            dst_ref=wbuf.at[where, cols],
            send_sem=core_send.at[c, number[offset]],
            recv_sem=core_recv.at[c, number[offset]],
            device_id=other,
            device_id_type=MESH,
        )

    def core_arrived(c, offset):
        dz, da, db = offset
        at, width = chunks[c]
        theirs = 1 - core
        dx = da * (1 - theirs) + db * theirs
        dy = da * theirs + db * (1 - theirs)
        device = ((z + dz) % nz) * n + (x + dx) % n, ((y + dy) % n) * 2 + theirs
        ref = wbuf.at[rows_of(device), pl.ds(at, width)]
        pltpu.make_async_copy(ref, ref, core_recv.at[c, number[offset]]).wait()

    def start(copy):
        copy.start()
        sends.append(copy)

    def send_on(c, offset):
        if offset[1] == 0 and offset[2] == 0:
            for da in range(1, n):
                start(link_copy(c, offset, (0, da, 0)))
        if offset[2] == 0:
            for db in range(1, n):
                start(link_copy(c, offset, (0, 0, db)))
        start(core_copy(c, offset))

    def send_own(c):
        for dz in range(1, nz):
            start(link_copy(c, (0, 0, 0), (dz, 0, 0)))
        send_on(c, (0, 0, 0))

    def forward(c):
        order = sorted(offsets[1:], key=lambda o: (o[2] > 0, o[1] > 0))
        for offset in order:
            arrived(c, offset)
            send_on(c, offset)

    def multiply(c):
        for offset in offsets:
            core_arrived(c, offset)
        at, width = chunks[c]
        if at < inner:

            @pl.loop(0, width // 256)
            def _(tile):
                cols = pl.ds(pl.multiple_of(at + tile * 256, 256), 256)
                raw_ref[:, cols] = dot(ext[...], wbuf[:, cols]).astype(BF16)

        else:
            mid = at + 2 * STATE
            raw_ref[:, at:mid] = dot(ext[...], wbuf[:, at:mid]).astype(BF16)
            step_ref[...] = dot(ext[...], wbuf[:, mid:])

    send_own(0)
    rim.start()
    tokens_in = pltpu.make_async_copy(tok_ref, ext.at[pl.ds(RIM, count)], tok_sem.at[0])
    tokens_in.start()
    own_in = pltpu.make_async_copy(w_ref, wbuf.at[own_rows], own_sem.at[0])
    own_in.start()
    send_own(1)
    rim.wait()
    tokens_in.wait()
    own_in.wait()

    @pl.when(seq == 0)
    def _():
        ext[0:RIM, :] = jnp.zeros((RIM, ext.shape[1]), BF16)

    for c in range(len(chunks)):
        forward(c)
        if c + 2 < len(chunks):
            send_own(c + 2)
        if c > 0:
            multiply(c - 1)
    multiply(len(chunks) - 1)
    for copy in sends:
        copy.wait_send()


def project(tokens, w_in, inner, nseq, ndp):
    count, depth = tokens.shape
    rows, width = w_in.shape
    padded = -(-width // LANES) * LANES
    n = ndp // 2
    nz = nseq // n
    w_in = jnp.pad(w_in, ((0, 0), (0, padded - width)))
    channels = inner + 2 * STATE
    if nseq * ndp > 32:
        before = lax.ppermute(tokens[count - RIM :], "seq", [(i, i + 1) for i in range(nseq - 1)])
        full = lax.all_gather(w_in, ("seq", "dp"), axis=0, tiled=True)
        out = jnp.dot(jnp.concatenate([before, tokens], 0), full, preferred_element_type=F32)
        return out[:, :channels].astype(BF16), out[:, channels:]
    total = count + RIM
    shards = nz * n * n
    chunks = len(chunk_list(inner, padded))
    return pl.pallas_call(
        functools.partial(project_kernel, nz, n, inner),
        out_shape=(
            jax.ShapeDtypeStruct((total, channels), BF16),
            jax.ShapeDtypeStruct((total, padded - channels), F32),
        ),
        in_specs=[pl.BlockSpec(memory_space=pl.ANY)] * 2,
        out_specs=(pl.BlockSpec(memory_space=pltpu.VMEM),) * 2,
        scratch_shapes=[
            pltpu.VMEM((total, depth), BF16),
            pltpu.VMEM((depth, padded), BF16),
            pltpu.SemaphoreType.DMA((1,)),
            pltpu.SemaphoreType.DMA((2,)),
            pltpu.SemaphoreType.DMA((1,)),
            pltpu.SemaphoreType.DMA((chunks, shards)),
            pltpu.SemaphoreType.DMA((chunks, shards)),
            pltpu.SemaphoreType.DMA((chunks, shards)),
            pltpu.SemaphoreType.DMA((chunks, shards)),
        ],
        compiler_params=pltpu.CompilerParams(
            collective_id=0, has_side_effects=True, vmem_limit_bytes=48 * 2**20
        ),
        name="project",
    )(tokens, w_in)


def split_terms(value, terms):
    parts = []
    for _ in range(terms):
        part = value.astype(BF16)
        parts.append(part)
        value = value - part.astype(F32)
    return parts


def expander(chunk, terms):
    head = lax.broadcasted_iota(jnp.int32, (LANES, WIDE), 0)
    lane = lax.broadcasted_iota(jnp.int32, (LANES, WIDE), 1)
    heads = WIDE // HEAD
    one = jnp.where(head == chunk * heads + lane // HEAD, 1.0, 0.0).astype(BF16)
    return jnp.concatenate([one] * terms, 0)


def expand(value, chunk, terms=2):
    return dot(jnp.concatenate(split_terms(value, terms), 1), expander(chunk, terms))


def convolve(raw, conv_ref, padded_ref, count):
    padded_ref[...] = raw.astype(F32)
    total = jnp.zeros((count, raw.shape[1]), F32)
    for tap in range(4):
        total = total + padded_ref[pl.ds(RIM - 3 + tap, count), :] * conv_ref[tap : tap + 1, :]
    return total


def mix_kernel(
    level_ref, raw_ref, bc_ref, step_ref, conv_ref, conv_bc_ref, rate_ref, skip_ref,
    y_ref, state_ref, sums_ref, reach_ref, query_ref,
    keys_t, cumul_s, cumul_t, scores_s, ends_s, steps_s, padded_s, padded_bc, totals_s,
):
    chunk = pl.program_id(0)
    count = y_ref.shape[0]
    stretches = count // Q
    pairs = count // LANES
    row = lax.broadcasted_iota(jnp.int32, (LANES, LANES), 0)
    col = lax.broadcasted_iota(jnp.int32, (LANES, LANES), 1)
    causal = (col <= row) & (row // Q == col // Q)

    def level(at):
        return level_ref[0, at].astype(F32) / 256.0

    @pl.when(chunk == 0)
    def _():
        both = convolve(bc_ref[...], conv_bc_ref, padded_bc, count)
        keys = both[:, :STATE].astype(BF16)
        query = both[:, STATE:].astype(BF16)
        query_ref[...] = query
        steps = step_ref[pl.ds(RIM, count), :]
        steps = jnp.maximum(steps, 0.0) + jnp.log1p(jnp.exp(-jnp.abs(steps)))
        steps_s[...] = steps
        decay = -steps * rate_ref[...]
        ones = jnp.where(causal, 1.0, 0.0).astype(BF16)
        before = jnp.zeros((1, LANES), F32)
        totals_s[...] = jnp.zeros_like(totals_s)
        for p in range(pairs):
            rows = slice(p * LANES, (p + 1) * LANES)
            terms = split_terms(decay[rows], 3)
            cumul = dot(ones, terms[2]) + dot(ones, terms[1]) + dot(ones, terms[0])
            cumul_s[rows, :] = cumul
            cumul_t[:, rows] = cumul.T
            keys_p = keys[rows].astype(F32).T.astype(BF16)
            keys_t[:, rows] = keys_p
            scores_s[rows, :] = dot(query[rows], keys_p) * level(0)
            for half in range(2):
                part = cumul[half * Q : (half + 1) * Q]
                total = part[Q - 1 : Q]
                at = slice(p * LANES + half * Q, p * LANES + (half + 1) * Q)
                ends_s[at, :] = jnp.exp(total - part)
                reach_ref[at, :] = jnp.exp(part + before)
                totals_s[2 * p + half : 2 * p + half + 1, :] = total
                before = before + total
        sums_ref[...] = jnp.broadcast_to(before, sums_ref.shape)

    convolved = convolve(raw_ref[...], conv_ref, padded_s, count)
    values = (convolved / (1.0 + jnp.exp(-convolved))).astype(BF16).astype(F32)
    driven_f = values * expand(steps_s[...], chunk, 3)
    driven = driven_f.astype(BF16)
    ended = (driven.astype(F32) * expand(ends_s[...], chunk)).astype(BF16)
    totals = expand(totals_s[...], chunk, 3)
    heads = WIDE // HEAD
    turn = (LANES - chunk * heads) % LANES
    left = lax.broadcasted_iota(jnp.int32, (LANES, LANES), 1) < HEAD
    upper = lax.broadcasted_iota(jnp.int32, (LANES, WIDE), 0) < Q
    states = []
    for p in range(pairs):
        rows = slice(p * LANES, (p + 1) * LANES)
        down = pltpu.roll(cumul_s[rows, :], turn, 1)
        along = cumul_t[pl.ds(pl.multiple_of(chunk * heads, heads), heads), rows]
        scores = scores_s[rows, :]
        for two in range(heads // 2):
            cols = slice(two * LANES, (two + 1) * LANES)
            parts = []
            for h in (2 * two, 2 * two + 1):
                differ = down[:, h : h + 1] - along[h : h + 1, :]
                weight = jnp.exp(jnp.where(causal, differ, -1e30)) * scores
                parts.append(dot(weight.astype(BF16), driven[rows, cols]))
            y_ref[rows, cols] = (
                jnp.where(left, parts[0], parts[1]) + skip_ref[:, cols] * values[rows, cols]
            )
        ended_p = ended[rows]
        keys_p = keys_t[:, rows]
        zero = jnp.zeros_like(ended_p)
        states.append(dot(keys_p, jnp.where(upper, ended_p, zero)))
        states.append(dot(keys_p, jnp.where(upper, zero, ended_p)))

    sums = [totals[i : i + 1] for i in range(stretches)]
    carried = [None] * stretches
    blocks, block_sums = states, sums
    bits = stretches.bit_length() - 1
    for bit in range(bits):
        weight = level(bit + 1)
        for k in range(1, len(blocks), 2):
            passed = jnp.zeros((1, WIDE), F32)
            for j in range(k << bit, (k + 1) << bit):
                term = blocks[k - 1] * (weight * jnp.exp(passed))
                carried[j] = term if carried[j] is None else carried[j] + term
                passed = passed + sums[j]
        merged = [
            blocks[k] * jnp.exp(block_sums[k + 1]) + blocks[k + 1] for k in range(0, len(blocks), 2)
        ]
        block_sums = [block_sums[k] + block_sums[k + 1] for k in range(0, len(blocks), 2)]
        blocks = merged
    state_ref[...] = blocks[0].astype(BF16)
    for j in range(1, stretches):
        rows = slice(j * Q, (j + 1) * Q)
        grown = expand(jnp.exp(cumul_s[rows, :]), chunk)
        y_ref[rows, :] += grown * dot(query_ref[rows, :], carried[j].astype(BF16))


def mix(raw, steps, conv_w, rate, skip, level_w, count):
    inner = conv_w.shape[1] - 2 * STATE
    total = raw.shape[0]
    whole = lambda shape: pl.BlockSpec(shape, lambda i: (0, 0))
    part = lambda rows: pl.BlockSpec((rows, WIDE), lambda i: (0, i))
    tail = lambda rows: pl.BlockSpec((rows, 2 * STATE), lambda i: (0, inner // (2 * STATE)))
    return pl.pallas_call(
        mix_kernel,
        grid=(inner // WIDE,),
        in_specs=[
            pl.BlockSpec(memory_space=pltpu.SMEM),
            part(total),
            tail(total),
            whole((total, LANES)),
            part(4),
            tail(4),
            whole((1, LANES)),
            part(1),
        ],
        out_specs=(part(count), part(STATE), whole((8, LANES)), whole((count, LANES)), whole((count, STATE))),
        out_shape=(
            jax.ShapeDtypeStruct((count, inner), F32),
            jax.ShapeDtypeStruct((STATE, inner), BF16),
            jax.ShapeDtypeStruct((8, LANES), F32),
            jax.ShapeDtypeStruct((count, LANES), F32),
            jax.ShapeDtypeStruct((count, STATE), BF16),
        ),
        scratch_shapes=[
            pltpu.VMEM((STATE, count), BF16),
            pltpu.VMEM((count, LANES), F32),
            pltpu.VMEM((LANES, count), F32),
            pltpu.VMEM((count, LANES), F32),
            pltpu.VMEM((count, LANES), F32),
            pltpu.VMEM((count, LANES), F32),
            pltpu.VMEM((total, WIDE), F32),
            pltpu.VMEM((total, 2 * STATE), F32),
            pltpu.VMEM((max(8, count // Q), LANES), F32),
        ],
        compiler_params=pltpu.CompilerParams(vmem_limit_bytes=48 * 2**20),
        name="mix",
    )(level_w, raw, raw, steps, conv_w, conv_w, rate, skip)


def finish_kernel(live_ref, y_ref, cross_ref, reach_ref, query_ref, out_ref):
    chunk = pl.program_id(0)
    count = y_ref.shape[0]
    output = y_ref[...] + expand(reach_ref[...], chunk) * dot(query_ref[...], cross_ref[...])
    squares = output * output
    row = lax.broadcasted_iota(jnp.int32, (LANES, LANES), 0)
    col = lax.broadcasted_iota(jnp.int32, (LANES, LANES), 1)
    same = jnp.where(row // HEAD == col // HEAD, 1.0 / HEAD, 0.0).astype(BF16)
    same = jnp.concatenate([same, same], 0)
    places = lax.broadcasted_iota(jnp.int32, (count, LANES), 0)
    live = places < live_ref[0]
    for two in range(WIDE // LANES):
        cols = slice(two * LANES, (two + 1) * LANES)
        mean = dot(jnp.concatenate(split_terms(squares[:, cols], 2), 1), same)
        out_ref[:, cols] = jnp.where(live, output[:, cols] * lax.rsqrt(mean + 1e-05), 0.0).astype(BF16)


def finish(live, y, cross, reach, query):
    count, inner = y.shape
    whole = lambda shape: pl.BlockSpec(shape, lambda i: (0, 0))
    part = lambda rows: pl.BlockSpec((rows, WIDE), lambda i: (0, i))
    return pl.pallas_call(
        finish_kernel,
        grid=(inner // WIDE,),
        in_specs=[
            pl.BlockSpec(memory_space=pltpu.SMEM),
            part(count),
            part(STATE),
            whole((count, LANES)),
            whole((count, STATE)),
        ],
        out_specs=part(count),
        out_shape=jax.ShapeDtypeStruct((count, inner), BF16),
        compiler_params=pltpu.CompilerParams(vmem_limit_bytes=48 * 2**20),
        name="finish",
    )(live, y, cross, reach, query)


def swapped(value, axis, stride):
    mask = 2**stride
    pairs = [(source, source ^ mask) for source in range(lax.axis_size(axis))]
    return lax.ppermute(value, axis, pairs)


def body(tokens, w_in, conv_w, a_rate, d_skip, level_w, lengths):
    token_rows = tokens.reshape(-1, tokens.shape[-1])
    count = token_rows.shape[0]
    heads = a_rate.shape[0]
    inner = conv_w.shape[1] - 2 * STATE
    nseq = lax.axis_size("seq")
    raw, steps = project(token_rows, w_in, inner, nseq, lax.axis_size("dp"))
    rate = jnp.pad(a_rate[None, :], ((0, 0), (0, LANES - heads)))
    skip = jnp.repeat(d_skip, HEAD)[None, :]
    y, block_state, sums, reach, query = mix(raw, steps, conv_w, rate, skip, level_w, count)
    level_wt = level_w.reshape(-1).astype(F32) / 256.0
    position = lax.axis_index("seq")
    wide = lambda value: jnp.repeat(value, HEAD)[None, :]
    block_state = block_state.astype(F32)
    block_total = sums[0, :heads]
    cross_state = jnp.zeros_like(block_state)
    passed = jnp.zeros_like(block_total)
    local_bits = (count // Q).bit_length() - 1
    for level in range(nseq.bit_length() - 1):
        other_state = swapped(block_state.astype(BF16), "seq", level).astype(F32)
        other_total = swapped(block_total, "seq", level)
        upper = (jnp.right_shift(position, level) & 1).astype(F32)
        weight = upper * level_wt[local_bits + level + 1]
        cross_state = cross_state + weight * wide(jnp.exp(passed)) * other_state
        passed = passed + upper * other_total
        block_state = jnp.where(
            upper > 0.5,
            other_state * wide(jnp.exp(block_total)) + block_state,
            block_state * wide(jnp.exp(other_total)) + other_state,
        )
        block_total = block_total + other_total
    live = lengths - position * count
    out = finish(live, y, cross_state.astype(BF16), reach, query)
    return out.reshape(1, count, inner)


def solution(mesh):
    in_specs = (P("dp", "seq", None), P(("seq", "dp"), None), P(), P(), P(), P("dp", None), P("dp"))
    out_specs = P("dp", "seq", None)
    return jax.shard_map(body, mesh=mesh, in_specs=in_specs, out_specs=out_specs, check_vma=False)
```

time: 316 us -> 193 us (0.61)
  the two profiles are of different devices: /device:TPU:24 before, /device:TPU:4 now
where the time goes in v1:
time: 193 us
  Pallas kernels  133 us (69%)
  waiting for transfers between devices  37.9 us (20%)
  starting transfers between devices  12.9 us (7%)
  local copies, waits for them, and re-layouts  5.96 us (3%)
  between operations  2.64 us (1%)
    pallas_call x1, Pallas kernels, project(): pl.pallas_call(functools.partial(project_kernel, nz, n, inner), out_shape...  112 us
    ppermute x5, waiting for transfers between devices, swapped(): return lax.ppermute(value, axis, pairs)  37.9 us
    pallas_call x1, Pallas kernels, mix(): pl.pallas_call(mix_kernel, grid=(inner // WIDE,), in_specs=[pl.BlockSpec(...  16 us
    ppermute x5, starting transfers between devices, swapped(): return lax.ppermute(value, axis, pairs)  12.9 us
    pallas_call x1, Pallas kernels, finish(): pl.pallas_call(finish_kernel, grid=(inner // WIDE,), in_specs=[pl.BlockSp...  4.36 us
  transfers between devices with their start and end apart: 5, of which 4 were waited for; matrix products, arithmetic and copies ran while one was open for 1% of the time, Pallas kernels for 0%

profile of v1, /device:TPU:4, one launch (start us, length us, event | category | flops | bytes accessed | tf_op | source)
XLA Modules:
  0.0 193.2 jit_solution(12453014838069688272)
XLA Ops:
  0.0 0.0 copy-start.3
  0.0 0.0 copy-start.2
  0.0 0.0 copy-start.1
  0.0 1.4 copy.8
  1.4 0.7 broadcast_in_dim.25
  2.1 0.1 broadcast_in_dim_reshape.2.skip_ref
  2.3 112.4 %project.1 = (bf16[528,2304]{1,0:T(8,128)(2,1)S(1)}, f32[528,128]{1,0:T(8,128)S(1)}) custom-call(bf16[512,4096]{1,0:T(8,128)(2,1)} %bitcast.14, bf16[128,2432]{1,0:T(8,128)(2,1)S(1)} %pad.8.w_ref), custom_call_target="tpu_custom_call" | custom-call | tf_op jit(solution)/shard_map/project/pallas_call | solution.py:205
  114.6 0.0 copy-done.3
  114.7 0.0 copy-done.2
  114.7 0.0 copy-done.1
  114.7 16.0 %mix.1 = (f32[512,2048]{1,0:T(8,128)}, bf16[128,2048]{1,0:T(8,128)(2,1)S(1)}, f32[8,128]{1,0:T(8,128)S(1)}, f32[512,128]{1,0:T(8,128)S(1)}, bf16[512,128]{1,0:T(8,128)(2,1)S(1)}) custom-call(s32[1,11]{1,0:T(1,128)S(1)} %copy-done.2, bf16[528,2304]{1,0:T(8,128)(2,1)S(1)} %get-tuple-element.12.raw_ref.bc_ref, ...), custom_call_target="tpu_custom_call" | custom-call | tf_op jit(solution)/shard_map/mix/pallas_call | solution.py:370
  130.7 0.0 collective-permute-start.1
  130.7 2.0 %collective-permute-start = (bf16[128,2048]{1,0:T(8,128)(2,1)S(1)}, bf16[128,2048]{1,0:T(8,128)(2,1)S(1)}, u32[]{:S(2)}, u32[]{:S(2)}) collective-permute-start(bf16[128,2048]{1,0:T(8,128)(2,1)S(1)} %get-tuple-element.15), channel_id=1, source_target_pairs={{0,4},{4,0},{8,12},{12,8},{16,20},{20,16},{24,28},{28,24},{1,5},{5... | collective-permute-start | bytes 1572872 | tf_op jit(solution)/shard_map/ppermute | solution.py:448
  132.7 0.7 fusion.12
  134.6 0.0 collective-permute-done.1
  134.6 4.0 %collective-permute-start.3 = (f32[32]{0:T(128)S(1)}, f32[32]{0:T(128)S(1)}, u32[]{:S(2)}, u32[]{:S(2)}) collective-permute-start(f32[32]{0:T(128)S(1)} %get-tuple-element.20), channel_id=1, source_target_pairs={{0,8},{4,12},{8,0},{12,4},{16,24},{20,28},{24,16},{28,20},{1,9},{5... | collective-permute-start | bytes 392 | tf_op jit(solution)/shard_map/ppermute | solution.py:448
  138.6 0.1 broadcast_in_dim.27
  138.7 0.1 mul.123
  138.8 1.4 collective-permute-done.3
  140.2 0.1 broadcast_in_dim.28
  140.2 0.1 mul.126
  140.3 3.1 %collective-permute-done = bf16[128,2048]{1,0:T(8,128)(2,1)S(1)} collective-permute-done((bf16[128,2048]{1,0:T(8,128)(2,1)S(1)}, bf16[128,2048]{1,0:T(8,128)(2,1)S(1)}, u32[]{:S(2)}, u32[]{:S(2)}) %collective-permute-start) | collective-permute-done | bytes 524320 | tf_op jit(solution)/shard_map/ppermute | solution.py:448
  143.4 0.3 fusion.7
  143.7 6.8 %collective-permute-start.2 = (bf16[128,2048]{1,0:T(8,128)(2,1)S(1)}, bf16[128,2048]{1,0:T(8,128)(2,1)S(1)}, u32[]{:S(2)}, u32[]{:S(2)}) collective-permute-start(bf16[128,2048]{1,0:T(8,128)(2,1)S(1)} %fusion.7), channel_id=1, source_target_pairs={{0,8},{4,12},{8,0},{12,4},{16,24},{20,28},{24,16},{28,20},{1,9},{5... | collective-permute-start | bytes 1572872 | tf_op jit(solution)/shard_map/ppermute | solution.py:448
  150.5 0.1 broadcast_in_dim.30
  150.5 0.1 mul.137
  150.6 0.1 broadcast_in_dim.31
  150.7 0.1 mul.140
  150.8 10.8 %collective-permute-done.2 = bf16[128,2048]{1,0:T(8,128)(2,1)S(1)} collective-permute-done((bf16[128,2048]{1,0:T(8,128)(2,1)S(1)}, bf16[128,2048]{1,0:T(8,128)(2,1)S(1)}, u32[]{:S(2)}, u32[]{:S(2)}) %collective-permute-start.2) | collective-permute-done | bytes 524320 | tf_op jit(solution)/shard_map/ppermute | solution.py:448
  161.5 0.5 fusion.6
  162.0 0.1 collective-permute-start.4
  163.4 0.1 broadcast_in_dim.26
  163.4 0.1 mul.121
  163.5 0.1 broadcast_in_dim.29
  163.6 0.1 mul.135
  163.7 22.7 %collective-permute-done.4 = bf16[128,2048]{1,0:T(8,128)(2,1)S(1)} collective-permute-done((bf16[128,2048]{1,0:T(8,128)(2,1)S(1)}, bf16[128,2048]{1,0:T(8,128)(2,1)S(1)}, u32[]{:S(2)}, u32[]{:S(2)}) %collective-permute-start.4) | collective-permute-done | bytes 524320 | tf_op jit(solution)/shard_map/ppermute | solution.py:448
  186.3 0.3 fusion.3.cross_ref
  186.6 0.0 copy-start
  186.6 2.2 %copy-done = f32[512,2048]{1,0:T(8,128)S(1)} copy-done((f32[512,2048]{1,0:T(8,128)S(1)}, f32[512,2048]{1,0:T(8,128)}, u32[]{:S(2)}) %copy-start) | copy-done | bytes 4194328
  188.8 4.4 %finish.1 = bf16[512,2048]{1,0:T(8,128)(2,1)} custom-call(s32[1]{0:T(128)S(6)} %sub.7.live_ref, f32[512,2048]{1,0:T(8,128)S(1)} %copy-done, bf16[128,2048]{1,0:T(8,128)(2,1)S(1)} %fusion.3.cross_ref, f32[512,128]{1,0:T(8,128)S(1)} %get-tuple-element.17.reach_ref, bf16[512,128]{1,0:T(8,128)(2,1)S(1)} %get-tuple-element.18.query_ref), custom_call_target="tpu_custom_call" | custom-call | tf_op jit(solution)/shard_map/finish/pallas_call | solution.py:428
  (6 shorter events, 0.1 us)
Async XLA Ops:
  0.0 114.6 %copy-start.3 = (f32[32]{0:T(128)S(1)}, f32[32]{0:T(128)}, u32[]{:S(2)}) copy-start(f32[32]{0:T(128)} %param.10) | copy-start | bytes 388
  0.0 114.7 %copy-start.2 = (s32[1,11]{1,0:T(1,128)S(1)}, s32[1,11]{1,0:T(1,128)}, u32[]{:S(2)}) copy-start(s32[1,11]{1,0:T(1,128)} %level_ref.1) | copy-start | bytes 136
  0.0 114.7 %copy-start.1 = (f32[4,2304]{1,0:T(4,128)S(1)}, f32[4,2304]{1,0:T(4,128)}, u32[]{:S(2)}) copy-start(f32[4,2304]{1,0:T(4,128)} %conv_bc_ref.1) | copy-start | bytes 110596
  130.7 3.9 %collective-permute-start.1 = (f32[32]{0:T(128)S(1)}, f32[32]{0:T(128)S(1)}, u32[]{:S(2)}, u32[]{:S(2)}) collective-permute-start(f32[32]{0:T(128)S(1)} %slice_bitcast_fusion), channel_id=1, source_target_pairs={{0,4},{4,0},{8,12},{12,8},{16,20},{20,16},{24,28},{28,24},{1,5},{5... | collective-permute-start | bytes 392 | tf_op jit(solution)/shard_map/ppermute | solution.py:448
  130.7 12.7 %collective-permute-start = (bf16[128,2048]{1,0:T(8,128)(2,1)S(1)}, bf16[128,2048]{1,0:T(8,128)(2,1)S(1)}, u32[]{:S(2)}, u32[]{:S(2)}) collective-permute-start(bf16[128,2048]{1,0:T(8,128)(2,1)S(1)} %get-tuple-element.15), channel_id=1, source_target_pairs={{0,4},{4,0},{8,12},{12,8},{16,20},{20,16},{24,28},{28,24},{1,5},{5... | collective-permute-start | bytes 1572872 | tf_op jit(solution)/shard_map/ppermute | solution.py:448
  134.6 5.5 %collective-permute-start.3 = (f32[32]{0:T(128)S(1)}, f32[32]{0:T(128)S(1)}, u32[]{:S(2)}, u32[]{:S(2)}) collective-permute-start(f32[32]{0:T(128)S(1)} %get-tuple-element.20), channel_id=1, source_target_pairs={{0,8},{4,12},{8,0},{12,4},{16,24},{20,28},{24,16},{28,20},{1,9},{5... | collective-permute-start | bytes 392 | tf_op jit(solution)/shard_map/ppermute | solution.py:448
  143.7 17.8 %collective-permute-start.2 = (bf16[128,2048]{1,0:T(8,128)(2,1)S(1)}, bf16[128,2048]{1,0:T(8,128)(2,1)S(1)}, u32[]{:S(2)}, u32[]{:S(2)}) collective-permute-start(bf16[128,2048]{1,0:T(8,128)(2,1)S(1)} %fusion.7), channel_id=1, source_target_pairs={{0,8},{4,12},{8,0},{12,4},{16,24},{20,28},{24,16},{28,20},{1,9},{5... | collective-permute-start | bytes 1572872 | tf_op jit(solution)/shard_map/ppermute | solution.py:448
  162.0 24.3 %collective-permute-start.4 = (bf16[128,2048]{1,0:T(8,128)(2,1)S(1)}, bf16[128,2048]{1,0:T(8,128)(2,1)S(1)}, u32[]{:S(2)}, u32[]{:S(2)}) collective-permute-start(bf16[128,2048]{1,0:T(8,128)(2,1)S(1)} %fusion.6), channel_id=1, source_target_pairs={{0,16},{4,20},{8,24},{12,28},{16,0},{20,4},{24,8},{28,12},{1,17},{... | collective-permute-start | bytes 1572872 | tf_op jit(solution)/shard_map/ppermute | solution.py:448
  186.6 2.2 %copy-start = (f32[512,2048]{1,0:T(8,128)S(1)}, f32[512,2048]{1,0:T(8,128)}, u32[]{:S(2)}) copy-start(f32[512,2048]{1,0:T(8,128)} %get-tuple-element.14.y_ref) | copy-start | bytes 12582916

commit v2 on v1

v2 whole, which is shorter than its diff:
```python
import functools

import jax
import jax.numpy as jnp
from jax import lax
from jax.experimental import pallas as pl
from jax.experimental.pallas import tpu as pltpu
from jax.sharding import PartitionSpec as P

STATE = 128
Q = 64
RIM = 16
LANES = 128
WIDE = 512
HEAD = 64
MESH = pl.DeviceIdType.MESH
F32 = jnp.float32
BF16 = jnp.bfloat16


def dot(a, b):
    return jnp.dot(a, b, preferred_element_type=F32)


def chunk_list(inner, padded):
    chunks = [(inner, padded - inner)]
    at = 0
    while at < inner:
        width = WIDE if inner - at > WIDE else WIDE // 2
        chunks.append((at, width))
        at += width
    return chunks


def split_terms(value, terms):
    parts = []
    for _ in range(terms):
        part = value.astype(BF16)
        parts.append(part)
        value = value - part.astype(F32)
    return parts


def expand(value, first, width, terms=2):
    head = lax.broadcasted_iota(jnp.int32, (LANES, width), 0)
    lane = lax.broadcasted_iota(jnp.int32, (LANES, width), 1)
    one = jnp.where(head == first + lane // HEAD, 1.0, 0.0).astype(BF16)
    return dot(jnp.concatenate(split_terms(value, terms), 1), jnp.concatenate([one] * terms, 0))


def convolve(padded_ref, conv_ref, count):
    total = jnp.zeros((count, padded_ref.shape[1]), F32)
    for tap in range(4):
        total = total + padded_ref[pl.ds(RIM - 3 + tap, count), :] * conv_ref[tap : tap + 1, :]
    return total


def causal_mask():
    row = lax.broadcasted_iota(jnp.int32, (LANES, LANES), 0)
    col = lax.broadcasted_iota(jnp.int32, (LANES, LANES), 1)
    return (col <= row) & (row // Q == col // Q)


def prepare(level, padded_bc, steps, conv_bc, rate, query_ref, sums_ref, reach_ref, local):
    keys_t, cumul_s, cumul_t, scores_s, ends_s, steps_s, totals_s = local
    count = query_ref.shape[0]
    both = convolve(padded_bc, conv_bc, count)
    keys = both[:, :STATE].astype(BF16)
    query = both[:, STATE:].astype(BF16)
    query_ref[...] = query
    steps = jnp.maximum(steps, 0.0) + jnp.log1p(jnp.exp(-jnp.abs(steps)))
    steps_s[...] = steps
    decay = -steps * rate
    ones = jnp.where(causal_mask(), 1.0, 0.0).astype(BF16)
    before = jnp.zeros((1, LANES), F32)
    totals_s[...] = jnp.zeros_like(totals_s)
    for p in range(count // LANES):
        rows = slice(p * LANES, (p + 1) * LANES)
        terms = split_terms(decay[rows], 3)
        cumul = dot(ones, terms[2]) + dot(ones, terms[1]) + dot(ones, terms[0])
        cumul_s[rows, :] = cumul
        cumul_t[:, rows] = cumul.T
        keys_p = keys[rows].astype(F32).T.astype(BF16)
        keys_t[:, rows] = keys_p
        scores_s[rows, :] = dot(query[rows], keys_p) * level(0)
        for half in range(2):
            part = cumul[half * Q : (half + 1) * Q]
            total = part[Q - 1 : Q]
            at = slice(p * LANES + half * Q, p * LANES + (half + 1) * Q)
            ends_s[at, :] = jnp.exp(total - part)
            reach_ref[at, :] = jnp.exp(part + before)
            totals_s[2 * p + half : 2 * p + half + 1, :] = total
            before = before + total
    sums_ref[...] = jnp.broadcast_to(before, sums_ref.shape)


def mix_chunk(level, first, padded_s, conv_ref, skip, y_ref, query_ref, local):
    keys_t, cumul_s, cumul_t, scores_s, ends_s, steps_s, totals_s = local
    count, width = y_ref.shape
    stretches = count // Q
    pairs = count // LANES
    causal = causal_mask()
    convolved = convolve(padded_s, conv_ref, count)
    values = (convolved / (1.0 + jnp.exp(-convolved))).astype(BF16).astype(F32)
    driven = (values * expand(steps_s[...], first, width, 3)).astype(BF16)
    ended = (driven.astype(F32) * expand(ends_s[...], first, width)).astype(BF16)
    totals = expand(totals_s[...], first, width, 3)
    heads = width // HEAD
    turn = (LANES - first) % LANES
    left = lax.broadcasted_iota(jnp.int32, (LANES, LANES), 1) < HEAD
    upper = lax.broadcasted_iota(jnp.int32, (LANES, width), 0) < Q
    if not isinstance(first, int):
        first = pl.multiple_of(first, heads)
    states = []
    for p in range(pairs):
        rows = slice(p * LANES, (p + 1) * LANES)
        down = pltpu.roll(cumul_s[rows, :], turn, 1)
        along = cumul_t[pl.ds(first, heads), rows]
        scores = scores_s[rows, :]
        for two in range(heads // 2):
            cols = slice(two * LANES, (two + 1) * LANES)
            parts = []
            for h in (2 * two, 2 * two + 1):
                differ = down[:, h : h + 1] - along[h : h + 1, :]
                weight = jnp.exp(jnp.where(causal, differ, -1e30)) * scores
                parts.append(dot(weight.astype(BF16), driven[rows, cols]))
            y_ref[rows, cols] = (
                jnp.where(left, parts[0], parts[1]) + skip[:, cols] * values[rows, cols]
            )
        ended_p = ended[rows]
        keys_p = keys_t[:, rows]
        zero = jnp.zeros_like(ended_p)
        states.append(dot(keys_p, jnp.where(upper, ended_p, zero)))
        states.append(dot(keys_p, jnp.where(upper, zero, ended_p)))

    sums = [totals[i : i + 1] for i in range(stretches)]
    carried = [None] * stretches
    blocks, block_sums = states, sums
    for bit in range(stretches.bit_length() - 1):
        weight = level(bit + 1)
        for k in range(1, len(blocks), 2):
            passed = jnp.zeros((1, width), F32)
            for j in range(k << bit, (k + 1) << bit):
                term = blocks[k - 1] * (weight * jnp.exp(passed))
                carried[j] = term if carried[j] is None else carried[j] + term
                passed = passed + sums[j]
        merged = [
            blocks[k] * jnp.exp(block_sums[k + 1]) + blocks[k + 1] for k in range(0, len(blocks), 2)
        ]
        block_sums = [block_sums[k] + block_sums[k + 1] for k in range(0, len(blocks), 2)]
        blocks = merged
    grown = expand(jnp.exp(cumul_s[...]), first, width)
    for j in range(1, stretches):
        rows = slice(j * Q, (j + 1) * Q)
        y_ref[rows, :] += grown[rows] * dot(query_ref[rows, :], carried[j].astype(BF16))
    return blocks[0]


def finish_chunk(first, live_to, y, cross, reach_ref, query_ref, out_ref):
    count, width = out_ref.shape
    output = y + expand(reach_ref[...], first, width) * dot(query_ref[...], cross)
    squares = output * output
    row = lax.broadcasted_iota(jnp.int32, (LANES, LANES), 0)
    col = lax.broadcasted_iota(jnp.int32, (LANES, LANES), 1)
    same = jnp.where(row // HEAD == col // HEAD, 1.0 / HEAD, 0.0).astype(BF16)
    same = jnp.concatenate([same, same], 0)
    live = lax.broadcasted_iota(jnp.int32, (count, LANES), 0) < live_to
    for two in range(width // LANES):
        cols = slice(two * LANES, (two + 1) * LANES)
        mean = dot(jnp.concatenate(split_terms(squares[:, cols], 2), 1), same)
        out_ref[:, cols] = jnp.where(live, output[:, cols] * lax.rsqrt(mean + 1e-05), 0.0).astype(BF16)


def local_scratch(count):
    return [
        pltpu.VMEM((STATE, count), BF16),
        pltpu.VMEM((count, LANES), F32),
        pltpu.VMEM((LANES, count), F32),
        pltpu.VMEM((count, LANES), F32),
        pltpu.VMEM((count, LANES), F32),
        pltpu.VMEM((count, LANES), F32),
        pltpu.VMEM((max(8, count // Q), LANES), F32),
    ]


def mix_kernel(
    level_ref, raw_ref, bc_ref, step_ref, conv_ref, conv_bc_ref, rate_ref, skip_ref,
    y_ref, state_ref, sums_ref, reach_ref, query_ref, padded_s, padded_bc, *local,
):
    chunk = pl.program_id(0)
    level = lambda at: level_ref[0, at].astype(F32) / 256.0

    @pl.when(chunk == 0)
    def _():
        padded_bc[...] = bc_ref[...].astype(F32)
        steps = step_ref[pl.ds(RIM, y_ref.shape[0]), :]
        prepare(level, padded_bc, steps, conv_bc_ref, rate_ref[...], query_ref, sums_ref, reach_ref, local)

    padded_s[...] = raw_ref[...].astype(F32)
    first = chunk * (WIDE // HEAD)
    state = mix_chunk(level, first, padded_s, conv_ref, skip_ref[...], y_ref, query_ref, local)
    state_ref[...] = state.astype(BF16)


def mix(raw, steps, conv_w, rate, skip, level_w, count):
    inner = conv_w.shape[1] - 2 * STATE
    total = raw.shape[0]
    whole = lambda shape: pl.BlockSpec(shape, lambda i: (0, 0))
    part = lambda rows: pl.BlockSpec((rows, WIDE), lambda i: (0, i))
    tail = lambda rows: pl.BlockSpec((rows, 2 * STATE), lambda i: (0, inner // (2 * STATE)))
    return pl.pallas_call(
        mix_kernel,
        grid=(inner // WIDE,),
        in_specs=[
            pl.BlockSpec(memory_space=pltpu.SMEM),
            part(total),
            tail(total),
            whole((total, LANES)),
            part(4),
            tail(4),
            whole((1, LANES)),
            part(1),
        ],
        out_specs=(part(count), part(STATE), whole((8, LANES)), whole((count, LANES)), whole((count, STATE))),
        out_shape=(
            jax.ShapeDtypeStruct((count, inner), F32),
            jax.ShapeDtypeStruct((STATE, inner), BF16),
            jax.ShapeDtypeStruct((8, LANES), F32),
            jax.ShapeDtypeStruct((count, LANES), F32),
            jax.ShapeDtypeStruct((count, STATE), BF16),
        ),
        scratch_shapes=[
            pltpu.VMEM((total, WIDE), F32),
            pltpu.VMEM((total, 2 * STATE), F32),
        ]
        + local_scratch(count),
        compiler_params=pltpu.CompilerParams(vmem_limit_bytes=48 * 2**20),
        name="mix",
    )(level_w, raw, raw, steps, conv_w, conv_w, rate, skip)


def finish_kernel(live_ref, y_ref, cross_ref, reach_ref, query_ref, out_ref):
    first = pl.program_id(0) * (WIDE // HEAD)
    finish_chunk(first, live_ref[0], y_ref[...], cross_ref[...], reach_ref, query_ref, out_ref)


def finish(live, y, cross, reach, query):
    count, inner = y.shape
    whole = lambda shape: pl.BlockSpec(shape, lambda i: (0, 0))
    part = lambda rows: pl.BlockSpec((rows, WIDE), lambda i: (0, i))
    return pl.pallas_call(
        finish_kernel,
        grid=(inner // WIDE,),
        in_specs=[
            pl.BlockSpec(memory_space=pltpu.SMEM),
            part(count),
            part(STATE),
            whole((count, LANES)),
            whole((count, STATE)),
        ],
        out_specs=part(count),
        out_shape=jax.ShapeDtypeStruct((count, inner), BF16),
        compiler_params=pltpu.CompilerParams(vmem_limit_bytes=48 * 2**20),
        name="finish",
    )(live, y, cross, reach, query)


def swapped(value, axis, stride):
    mask = 2**stride
    pairs = [(source, source ^ mask) for source in range(lax.axis_size(axis))]
    return lax.ppermute(value, axis, pairs)


def fused_kernel(
    nz, n, inner, level_ref, live_ref, tok_ref, w_ref, conv_ref, rate_ref, skip_ref, out_ref,
    ext, wbuf, tok_sem, rim_sem, own_sem, send_sem, recv_sem, core_send, core_recv,
    y_s, out_s, padded_s, query_s, reach_s, sums_s, all_sums, own_state, pair_in, pair_state, quad_in,
    quad_state, third_in, cross_s, sum_send, sum_recv, state_send, state_recv, out_sem, *local,
):
    seq = lax.axis_index("seq")
    dp = lax.axis_index("dp")
    nseq = nz * n
    z, x = seq // n, seq % n
    y, core = dp // 2, dp % 2
    rows = w_ref.shape[0]
    count = tok_ref.shape[0]
    padded = w_ref.shape[1]
    chunks = chunk_list(inner, padded)
    after = (seq + 1) % nseq
    prior = (seq + nseq - 1) % nseq

    def place(dz, da, db):
        dx = da * (1 - core) + db * core
        dy = da * core + db * (1 - core)
        return ((z + dz) % nz) * n + (x + dx) % n, ((y + dy) % n) * 2 + core

    def rows_of(device):
        at = device[0] * (2 * n) + device[1]
        return pl.ds(pl.multiple_of(at * rows, rows), rows)

    offsets = [(dz, da, db) for dz in range(nz) for da in range(n) for db in range(n)]
    other = (seq, y * 2 + 1 - core)
    along_seq = [((seq + by) % nseq, dp) for by in range(1, nseq)]

    barrier = pltpu.get_barrier_semaphore()
    greeted = along_seq + [(seq, ((y + by) % n) * 2 + core) for by in range(1, n)] + [other]
    for device in greeted:
        pl.semaphore_signal(barrier, inc=1, device_id=device, device_id_type=MESH)
    pl.semaphore_wait(barrier, len(greeted))

    rim = pltpu.make_async_remote_copy(
        src_ref=tok_ref.at[pl.ds(count - RIM, RIM)],
        dst_ref=ext.at[pl.ds(0, RIM)],
        send_sem=rim_sem.at[0],
        recv_sem=rim_sem.at[1],
        device_id=(after, dp),
        device_id_type=MESH,
    )
    own_rows = rows_of((seq, dp))
    number = {offset: at for at, offset in enumerate(offsets)}
    sends = []

    def link_copy(c, offset, step):
        at, width = chunks[c]
        cols = pl.ds(at, width)
        where = rows_of(place(*offset))
        mine = offset == (0, 0, 0)
        lands = tuple((o - s) % m for o, s, m in zip(offset, step, (nz, n, n)))
        slot = number[lands]
        return pltpu.make_async_remote_copy(
            src_ref=w_ref.at[:, cols] if mine else wbuf.at[where, cols],
            dst_ref=wbuf.at[where, cols],
            send_sem=send_sem.at[c, slot],
            recv_sem=recv_sem.at[c, slot],
            device_id=place(*step),
            device_id_type=MESH,
        )

    def arrived(c, offset):
        at, width = chunks[c]
        ref = wbuf.at[rows_of(place(*offset)), pl.ds(at, width)]
        pltpu.make_async_copy(ref, ref, recv_sem.at[c, number[offset]]).wait()

    def core_copy(c, offset):
        at, width = chunks[c]
        cols = pl.ds(at, width)
        where = rows_of(place(*offset))
        mine = offset == (0, 0, 0)
        return pltpu.make_async_remote_copy(
            src_ref=w_ref.at[:, cols] if mine else wbuf.at[where, cols],
            dst_ref=wbuf.at[where, cols],
            send_sem=core_send.at[c, number[offset]],
            recv_sem=core_recv.at[c, number[offset]],
            device_id=other,
            device_id_type=MESH,
        )

    def core_arrived(c, offset):
        dz, da, db = offset
        at, width = chunks[c]
        theirs = 1 - core
        dx = da * (1 - theirs) + db * theirs
        dy = da * theirs + db * (1 - theirs)
        device = ((z + dz) % nz) * n + (x + dx) % n, ((y + dy) % n) * 2 + theirs
        ref = wbuf.at[rows_of(device), pl.ds(at, width)]
        pltpu.make_async_copy(ref, ref, core_recv.at[c, number[offset]]).wait()

    def start(copy):
        copy.start()
        sends.append(copy)

    def send_on(c, offset):
        if offset[1] == 0 and offset[2] == 0:
            for da in range(1, n):
                start(link_copy(c, offset, (0, da, 0)))
        if offset[2] == 0:
            for db in range(1, n):
                start(link_copy(c, offset, (0, 0, db)))
        start(core_copy(c, offset))

    def send_own(c):
        for dz in range(1, nz):
            start(link_copy(c, (0, 0, 0), (dz, 0, 0)))
        send_on(c, (0, 0, 0))

    def forward(c, stage):
        for offset in offsets[1:]:
            if (2 if offset[2] else 1 if offset[1] else 0) == stage:
                arrived(c, offset)
                send_on(c, offset)

    level = lambda at: level_ref[0, at].astype(F32) / 256.0
    bits = (count // Q).bit_length() - 1

    def sum_copy(by):
        return pltpu.make_async_remote_copy(
            src_ref=sums_s,
            dst_ref=all_sums.at[seq],
            send_sem=sum_send.at[by],
            recv_sem=sum_recv.at[by],
            device_id=((seq + by) % nseq, dp),
            device_id_type=MESH,
        )

    def multiply(c):
        for offset in offsets:
            core_arrived(c, offset)
        at, width = chunks[c]
        if c == 0:
            mid = at + 2 * STATE
            padded_s[:, 0 : 2 * STATE] = dot(ext[...], wbuf[:, at:mid]).astype(BF16).astype(F32)
            steps = dot(ext[...], wbuf[:, mid:])[RIM:]
            conv_bc = conv_ref.at[:, at:mid]
            prepare(
                level, padded_s.at[:, 0 : 2 * STATE], steps, conv_bc, rate_ref[...],
                query_s, sums_s, reach_s, local,
            )
            all_sums[seq] = sums_s[...]
            for by in range(1, nseq):
                sum_copy(by).start()
            return

        @pl.loop(0, width // 256)
        def _(tile):
            cols = pl.ds(pl.multiple_of(at + tile * 256, 256), 256)
            lands = pl.ds(pl.multiple_of(tile * 256, 256), 256)
            padded_s[:, lands] = dot(ext[...], wbuf[:, cols]).astype(BF16).astype(F32)

        cols = pl.ds(at, width)
        state = mix_chunk(
            level, at // HEAD, padded_s.at[:, 0:width], conv_ref.at[:, cols], skip_ref[:, cols],
            y_s.at[:, cols], query_s, local,
        )
        own_state[:, cols] = state.astype(BF16)
        state_copy(c, 0).start()

    def state_copy(c, hop):
        at, width = chunks[c]
        cols = pl.ds(at, width)
        source, target, device = (
            (own_state, pair_in, (seq + 1 - 2 * x, dp)),
            (pair_state, quad_in, ((seq + n) % nseq, dp)),
            (quad_state, quad_in, ((seq + n) % nseq, dp)),
            (quad_in, third_in, ((seq + n) % nseq, dp)),
        )[hop]
        return pltpu.make_async_remote_copy(
            src_ref=source.at[:, cols],
            dst_ref=target.at[:, cols],
            send_sem=state_send.at[c, hop],
            recv_sem=state_recv.at[c, hop],
            device_id=device,
            device_id_type=MESH,
        )

    def sums_of(c, device):
        at, width = chunks[c]
        return expand(all_sums[device], at // HEAD, width, 3)[0:1]

    upper = x.astype(F32)
    odd = z % 2

    def passed_pair(c):
        return upper * sums_of(c, z * n)

    def exchange(c, stage):
        at, width = chunks[c]
        cols = pl.ds(at, width)
        if stage == 0:
            state_copy(c, 0).wait_recv()
            mine = own_state[:, cols].astype(F32)
            theirs = pair_in[:, cols].astype(F32)
            cross_s[:, cols] = theirs * (upper * level(bits + 1))
            first = jnp.where(x == 0, mine, theirs)
            second = jnp.where(x == 0, theirs, mine)
            pair = first * jnp.exp(sums_of(c, z * n + 1)) + second
            pair_state[:, cols] = pair.astype(BF16)

            @pl.when(odd == 0)
            def _():
                state_copy(c, 1).start()

        elif stage == 1:

            @pl.when(odd == 1)
            def _():
                state_copy(c, 1).wait_recv()
                lower = quad_in[:, cols].astype(F32)
                cross_s[:, cols] += lower * (level(bits + 2) * jnp.exp(passed_pair(c)))
                pair_sum = sums_of(c, z * n) + sums_of(c, z * n + 1)
                quad = lower * jnp.exp(pair_sum) + pair_state[:, cols].astype(F32)
                quad_state[:, cols] = quad.astype(BF16)

            @pl.when(z == 1)
            def _():
                state_copy(c, 2).start()

        else:

            @pl.when(z == 2)
            def _():
                state_copy(c, 2).wait_recv()
                state_copy(c, 3).start()
                lower = quad_in[:, cols].astype(F32)
                cross_s[:, cols] += lower * (level(bits + 3) * jnp.exp(passed_pair(c)))

            @pl.when(z == 3)
            def _():
                state_copy(c, 3).wait_recv()
                lower = third_in[:, cols].astype(F32)
                before = passed_pair(c) + sums_of(c, z * n - 1) + sums_of(c, z * n - 2)
                cross_s[:, cols] += lower * (level(bits + 3) * jnp.exp(before))

            view = out_s.at[:, cols]
            finish_chunk(
                at // HEAD, live_ref[0], y_s[:, cols], cross_s[:, cols].astype(BF16), reach_s, query_s, view
            )
            out_copy(c).start()

    def out_copy(c):
        at, width = chunks[c]
        cols = pl.ds(at, width)
        return pltpu.make_async_copy(out_s.at[:, cols], out_ref.at[:, cols], out_sem.at[c])

    send_own(0)
    rim.start()
    tokens_in = pltpu.make_async_copy(tok_ref, ext.at[pl.ds(RIM, count)], tok_sem.at[0])
    tokens_in.start()
    own_in = pltpu.make_async_copy(w_ref, wbuf.at[own_rows], own_sem.at[0])
    own_in.start()
    send_own(1)
    rim.wait()
    tokens_in.wait()
    own_in.wait()

    @pl.when(seq == 0)
    def _():
        ext[0:RIM, :] = jnp.zeros((RIM, ext.shape[1]), BF16)

    last = len(chunks) - 1
    for step in range(last + 7):
        if step <= last:
            forward(step, 0)
        if step + 2 <= last:
            send_own(step + 2)
        if 0 <= step - 1 <= last:
            forward(step - 1, 1)
        if 0 <= step - 2 <= last:
            forward(step - 2, 2)
        for stage in (2, 1, 0):
            if 1 <= step - 4 - stage <= last:
                if step - 4 - stage == 1 and stage == 0:
                    for by in range(1, nseq):
                        sum_copy(by).wait_recv()
                exchange(step - 4 - stage, stage)
        if 0 <= step - 3 <= last:
            multiply(step - 3)
    for copy in sends:
        copy.wait_send()
    for by in range(1, nseq):
        sum_copy(by).wait_send()
    for c in range(1, last + 1):
        out_copy(c).wait()
        state_copy(c, 0).wait_send()

        @pl.when(odd == 0)
        def _():
            state_copy(c, 1).wait_send()

        @pl.when(z == 1)
        def _():
            state_copy(c, 2).wait_send()

        @pl.when(z == 2)
        def _():
            state_copy(c, 3).wait_send()


def fused(tokens, w_in, conv_w, rate, skip, level_w, live, nseq, ndp):
    count, depth = tokens.shape
    padded = -(-w_in.shape[1] // LANES) * LANES
    w_in = jnp.pad(w_in, ((0, 0), (0, padded - w_in.shape[1])))
    inner = conv_w.shape[1] - 2 * STATE
    n = ndp // 2
    nz = nseq // n
    total = count + RIM
    shards = nz * n * n
    chunks = len(chunk_list(inner, padded))
    smem = pl.BlockSpec(memory_space=pltpu.SMEM)
    vmem = pl.BlockSpec(memory_space=pltpu.VMEM)
    anywhere = pl.BlockSpec(memory_space=pl.ANY)
    state = pltpu.VMEM((STATE, inner), BF16)
    return pl.pallas_call(
        functools.partial(fused_kernel, nz, n, inner),
        out_shape=jax.ShapeDtypeStruct((count, inner), BF16),
        in_specs=[smem, smem, anywhere, anywhere, vmem, vmem, vmem],
        out_specs=anywhere,
        scratch_shapes=[
            pltpu.VMEM((total, depth), BF16),
            pltpu.VMEM((depth, padded), BF16),
            pltpu.SemaphoreType.DMA((1,)),
            pltpu.SemaphoreType.DMA((2,)),
            pltpu.SemaphoreType.DMA((1,)),
        ]
        + [pltpu.SemaphoreType.DMA((chunks, shards))] * 4
        + [
            pltpu.VMEM((count, inner), F32),
            pltpu.VMEM((count, inner), BF16),
            pltpu.VMEM((total, WIDE), F32),
            pltpu.VMEM((count, STATE), BF16),
            pltpu.VMEM((count, LANES), F32),
            pltpu.VMEM((8, LANES), F32),
            pltpu.VMEM((nseq, 8, LANES), F32),
        ]
        + [state] * 6
        + [
            pltpu.VMEM((STATE, inner), F32),
            pltpu.SemaphoreType.DMA((nseq,)),
            pltpu.SemaphoreType.DMA((nseq,)),
            pltpu.SemaphoreType.DMA((chunks, 4)),
            pltpu.SemaphoreType.DMA((chunks, 4)),
            pltpu.SemaphoreType.DMA((chunks,)),
        ]
        + local_scratch(count),
        compiler_params=pltpu.CompilerParams(
            collective_id=0, has_side_effects=True, vmem_limit_bytes=60 * 2**20
        ),
        name="fused",
    )(level_w, live, tokens, w_in, conv_w, rate, skip)


def body(tokens, w_in, conv_w, a_rate, d_skip, level_w, lengths):
    token_rows = tokens.reshape(-1, tokens.shape[-1])
    count = token_rows.shape[0]
    heads = a_rate.shape[0]
    inner = conv_w.shape[1] - 2 * STATE
    nseq = lax.axis_size("seq")
    rate = jnp.pad(a_rate[None, :], ((0, 0), (0, LANES - heads)))
    skip = jnp.repeat(d_skip, HEAD)[None, :]
    live = lengths - lax.axis_index("seq") * count
    ndp = lax.axis_size("dp")
    if (nseq, ndp) == (8, 4):
        out = fused(token_rows, w_in, conv_w, rate, skip, level_w, live, nseq, ndp)
        return out.reshape(1, count, inner)
    channels = conv_w.shape[1]
    edge = lax.ppermute(token_rows[count - RIM :], "seq", [(i, i + 1) for i in range(nseq - 1)])
    full = lax.all_gather(w_in, ("seq", "dp"), axis=0, tiled=True)
    projected = dot(jnp.concatenate([edge, token_rows], 0), full)
    raw = projected[:, :channels].astype(BF16)
    steps = jnp.pad(projected[:, channels:], ((0, 0), (0, LANES - heads)))
    y, block_state, sums, reach, query = mix(raw, steps, conv_w, rate, skip, level_w, count)
    level_wt = level_w.reshape(-1).astype(F32) / 256.0
    position = lax.axis_index("seq")
    wide = lambda value: jnp.repeat(value, HEAD)[None, :]
    block_state = block_state.astype(F32)
    block_total = sums[0, :heads]
    cross_state = jnp.zeros_like(block_state)
    passed = jnp.zeros_like(block_total)
    local_bits = (count // Q).bit_length() - 1
    for level in range(nseq.bit_length() - 1):
        other_state = swapped(block_state.astype(BF16), "seq", level).astype(F32)
        other_total = swapped(block_total, "seq", level)
        upper = (jnp.right_shift(position, level) & 1).astype(F32)
        weight = upper * level_wt[local_bits + level + 1]
        cross_state = cross_state + weight * wide(jnp.exp(passed)) * other_state
        passed = passed + upper * other_total
        block_state = jnp.where(
            upper > 0.5,
            other_state * wide(jnp.exp(block_total)) + block_state,
            block_state * wide(jnp.exp(other_total)) + other_state,
        )
        block_total = block_total + other_total
    out = finish(live, y, cross_state.astype(BF16), reach, query)
    return out.reshape(1, count, inner)


def solution(mesh):
    in_specs = (P("dp", "seq", None), P(("seq", "dp"), None), P(), P(), P(), P("dp", None), P("dp"))
    out_specs = P("dp", "seq", None)
    return jax.shard_map(body, mesh=mesh, in_specs=in_specs, out_specs=out_specs, check_vma=False)
```

time: 193 us -> 152 us (0.79)
  the two profiles are of different devices: /device:TPU:4 before, /device:TPU:24 now
where the time goes in v2:
time: 152 us; the launch traced here: 151 us
  Pallas kernels  143 us (94%)
  local copies, waits for them, and re-layouts  7.99 us (5%)
    pallas_call x1, Pallas kernels, fused(): pl.pallas_call(functools.partial(fused_kernel, nz, n, inner), out_shape=j...  143 us
    unnamed x2, local copies, waits for them, and re-layouts  4.52 us

profile of v2, /device:TPU:24, one launch (start us, length us, event | category | flops | bytes accessed | tf_op | source)
XLA Modules:
  0.0 151.2 jit_solution(3398699673846320633)
XLA Ops:
  0.7 1.2 pad.9.rate_ref
  1.9 0.7 broadcast_in_dim.7
  2.6 0.7 broadcast_in_dim_reshape.3.skip_ref
  3.3 1.4 copy.8
  4.6 0.9 pad.8.w_ref
  5.5 142.6 %fused.1 = bf16[512,2048]{1,0:T(8,128)(2,1)} custom-call(s32[1,11]{1,0:T(1,128)} %level_ref.1, s32[1]{0:T(128)S(6)} %sub.7.live_ref, bf16[512,4096]{1,0:T(8,128)(2,1)} %bitcast.5, bf16[128,2432]{1,0:T(8,128)(2,1)} %pad.8.w_ref, f32[4,2304]{1,0:T(4,128)} %conv_ref.1, f32[1,128]{1,0:T(1,128)} %pad.9.rate_ref, f32[1,2048]{1,0:T(1,128)} %broadcast_in_dim_reshape.3.skip_ref), custom_call_target="tpu_custom_call" | custom-call | tf_op jit(solution)/shard_map/fused/pallas_call | solution.py:592
  148.1 3.2 %copy.11 = bf16[1,512,2048]{2,1,0:T(8,128)(2,1)} copy(bf16[1,512,2048]{2,1,0:T(8,128)(2,1)} %bitcast.4) | data formatting | bytes 4194304

commit v3 on v2

--- a/solution.py
+++ b/solution.py
@@ -12,6 +12,7 @@
 RIM = 16
 LANES = 128
 WIDE = 512
+TURNED = 3
 HEAD = 64
 MESH = pl.DeviceIdType.MESH
 F32 = jnp.float32
@@ -26,7 +27,7 @@
     chunks = [(inner, padded - inner)]
     at = 0
     while at < inner:
-        width = WIDE if inner - at > WIDE else WIDE // 2
+        width = WIDE // 2 if inner - at <= WIDE // 2 or len(chunks) == TURNED else WIDE
         chunks.append((at, width))
         at += width
     return chunks
@@ -275,7 +276,7 @@
     nz, n, inner, level_ref, live_ref, tok_ref, w_ref, conv_ref, rate_ref, skip_ref, out_ref,
     ext, wbuf, tok_sem, rim_sem, own_sem, send_sem, recv_sem, core_send, core_recv,
     y_s, out_s, padded_s, query_s, reach_s, sums_s, all_sums, own_state, pair_in, pair_state, quad_in,
-    quad_state, third_in, cross_s, sum_send, sum_recv, state_send, state_recv, out_sem, *local,
+    quad_state, third_in, cross_s, sum_send, sum_recv, state_send, state_recv, out_sem, rates_s, *local,
 ):
     seq = lax.axis_index("seq")
     dp = lax.axis_index("dp")
@@ -369,23 +370,26 @@
         copy.start()
         sends.append(copy)
 
+    sizes = (nz, n, n)
+
+    def order_of(c):
+        return (1, 2, 0) if c == TURNED else (0, 1, 2)
+
+    def stage_of(c, offset):
+        return max([at for at, axis in enumerate(order_of(c)) if offset[axis]], default=-1)
+
     def send_on(c, offset):
-        if offset[1] == 0 and offset[2] == 0:
-            for da in range(1, n):
-                start(link_copy(c, offset, (0, da, 0)))
-        if offset[2] == 0:
-            for db in range(1, n):
-                start(link_copy(c, offset, (0, 0, db)))
+        for axis in order_of(c)[stage_of(c, offset) + 1 :]:
+            for by in range(1, sizes[axis]):
+                start(link_copy(c, offset, tuple(by if axis == at else 0 for at in range(3))))
         start(core_copy(c, offset))
 
     def send_own(c):
-        for dz in range(1, nz):
-            start(link_copy(c, (0, 0, 0), (dz, 0, 0)))
         send_on(c, (0, 0, 0))
 
     def forward(c, stage):
         for offset in offsets[1:]:
-            if (2 if offset[2] else 1 if offset[1] else 0) == stage:
+            if stage_of(c, offset) == stage:
                 arrived(c, offset)
                 send_on(c, offset)
 
@@ -412,7 +416,7 @@
             steps = dot(ext[...], wbuf[:, mid:])[RIM:]
             conv_bc = conv_ref.at[:, at:mid]
             prepare(
-                level, padded_s.at[:, 0 : 2 * STATE], steps, conv_bc, rate_ref[...],
+                level, padded_s.at[:, 0 : 2 * STATE], steps, conv_bc, rates_s[0:1],
                 query_s, sums_s, reach_s, local,
             )
             all_sums[seq] = sums_s[...]
@@ -428,7 +432,7 @@
 
         cols = pl.ds(at, width)
         state = mix_chunk(
-            level, at // HEAD, padded_s.at[:, 0:width], conv_ref.at[:, cols], skip_ref[:, cols],
+            level, at // HEAD, padded_s.at[:, 0:width], conv_ref.at[:, cols], expand(rates_s[1:2], at // HEAD, width, 3),
             y_s.at[:, cols], query_s, local,
         )
         own_state[:, cols] = state.astype(BF16)
@@ -528,32 +532,38 @@
     own_in = pltpu.make_async_copy(w_ref, wbuf.at[own_rows], own_sem.at[0])
     own_in.start()
     send_own(1)
-    rim.wait()
-    tokens_in.wait()
-    own_in.wait()
-
-    @pl.when(seq == 0)
-    def _():
-        ext[0:RIM, :] = jnp.zeros((RIM, ext.shape[1]), BF16)
+    send_own(2)
+    rates_s[...] = jnp.zeros_like(rates_s)
+    rates_s[0:1, 0 : rate_ref.shape[1]] = rate_ref[...]
+    rates_s[1:2, 0 : rate_ref.shape[1]] = skip_ref[...]
 
     last = len(chunks) - 1
     for step in range(last + 7):
         if step <= last:
             forward(step, 0)
-        if step + 2 <= last:
-            send_own(step + 2)
+        if step + 3 <= last:
+            send_own(step + 3)
         if 0 <= step - 1 <= last:
             forward(step - 1, 1)
-        if 0 <= step - 2 <= last:
-            forward(step - 2, 2)
-        for stage in (2, 1, 0):
+        if step == 3:
+            rim.wait()
+            tokens_in.wait()
+            own_in.wait()
+
+            @pl.when(seq == 0)
+            def _():
+                ext[0:RIM, :] = jnp.zeros((RIM, ext.shape[1]), BF16)
+
+        if 0 <= step - 3 <= last:
+            multiply(step - 3)
+        for stage in (0, 1, 2):
             if 1 <= step - 4 - stage <= last:
                 if step - 4 - stage == 1 and stage == 0:
                     for by in range(1, nseq):
                         sum_copy(by).wait_recv()
                 exchange(step - 4 - stage, stage)
-        if 0 <= step - 3 <= last:
-            multiply(step - 3)
+        if 0 <= step - 2 <= last:
+            forward(step - 2, 2)
     for copy in sends:
         copy.wait_send()
     for by in range(1, nseq):
@@ -619,6 +629,7 @@
             pltpu.SemaphoreType.DMA((chunks, 4)),
             pltpu.SemaphoreType.DMA((chunks, 4)),
             pltpu.SemaphoreType.DMA((chunks,)),
+            pltpu.VMEM((8, LANES), F32),
         ]
         + local_scratch(count),
         compiler_params=pltpu.CompilerParams(
@@ -634,13 +645,13 @@
     heads = a_rate.shape[0]
     inner = conv_w.shape[1] - 2 * STATE
     nseq = lax.axis_size("seq")
-    rate = jnp.pad(a_rate[None, :], ((0, 0), (0, LANES - heads)))
-    skip = jnp.repeat(d_skip, HEAD)[None, :]
     live = lengths - lax.axis_index("seq") * count
     ndp = lax.axis_size("dp")
     if (nseq, ndp) == (8, 4):
-        out = fused(token_rows, w_in, conv_w, rate, skip, level_w, live, nseq, ndp)
+        out = fused(token_rows, w_in, conv_w, a_rate[None, :], d_skip[None, :], level_w, live, nseq, ndp)
         return out.reshape(1, count, inner)
+    rate = jnp.pad(a_rate[None, :], ((0, 0), (0, LANES - heads)))
+    skip = jnp.repeat(d_skip, HEAD)[None, :]
     channels = conv_w.shape[1]
     edge = lax.ppermute(token_rows[count - RIM :], "seq", [(i, i + 1) for i in range(nseq - 1)])
     full = lax.all_gather(w_in, ("seq", "dp"), axis=0, tiled=True)

time: 152 us -> 140 us (0.921)
  Pallas kernels: 143 us -> 133 us
  local copies, waits for them, and re-layouts: 7.99 us -> 5.39 us
    pallas_call x1, Pallas kernels: 143 us -> 133 us  [fused(): pl.pallas_call(functools.partial(fused_kernel, nz, n, inner), out_shape=j...]
where the time goes in v3:
time: 140 us
  Pallas kernels  133 us (95%)
  local copies, waits for them, and re-layouts  5.39 us (4%)
    pallas_call x1, Pallas kernels, fused(): pl.pallas_call(functools.partial(fused_kernel, nz, n, inner), out_shape=j...  133 us
    unnamed x2, local copies, waits for them, and re-layouts  4.52 us

profile of v3, /device:TPU:24, one launch (start us, length us, event | category | flops | bytes accessed | tf_op | source)
XLA Modules:
  0.0 139.5 jit_solution(2283084381691785533)
XLA Ops:
  0.7 1.4 copy.8
  2.0 0.9 pad.4.w_ref
  2.9 133.5 %fused.1 = bf16[512,2048]{1,0:T(8,128)(2,1)} custom-call(s32[1,11]{1,0:T(1,128)} %level_ref.1, s32[1]{0:T(128)S(6)} %sub.7.live_ref, bf16[512,4096]{1,0:T(8,128)(2,1)} %bitcast.6, bf16[128,2432]{1,0:T(8,128)(2,1)} %pad.4.w_ref, f32[4,2304]{1,0:T(4,128)} %conv_ref.1, f32[1,32]{1,0:T(1,128)} %bitcast.7, f32[1,32]{1,0:T(1,128)} %bitcast.8), custom_call_target="tpu_custom_call" | custom-call | tf_op jit(solution)/shard_map/fused/pallas_call | solution.py:602
  136.4 3.2 %copy.11 = bf16[1,512,2048]{2,1,0:T(8,128)(2,1)} copy(bf16[1,512,2048]{2,1,0:T(8,128)(2,1)} %bitcast.5) | data formatting | bytes 4194304

commit v4 on v3

--- a/solution.py
+++ b/solution.py
@@ -276,7 +276,7 @@
     nz, n, inner, level_ref, live_ref, tok_ref, w_ref, conv_ref, rate_ref, skip_ref, out_ref,
     ext, wbuf, tok_sem, rim_sem, own_sem, send_sem, recv_sem, core_send, core_recv,
     y_s, out_s, padded_s, query_s, reach_s, sums_s, all_sums, own_state, pair_in, pair_state, quad_in,
-    quad_state, third_in, cross_s, sum_send, sum_recv, state_send, state_recv, out_sem, rates_s, *local,
+    quad_state, third_in, cross_s, sum_send, sum_recv, state_send, state_recv, out_sem, rates_s, skip_wide, sums_wide, *local,
 ):
     seq = lax.axis_index("seq")
     dp = lax.axis_index("dp")
@@ -432,7 +432,7 @@
 
         cols = pl.ds(at, width)
         state = mix_chunk(
-            level, at // HEAD, padded_s.at[:, 0:width], conv_ref.at[:, cols], expand(rates_s[1:2], at // HEAD, width, 3),
+            level, at // HEAD, padded_s.at[:, 0:width], conv_ref.at[:, cols], skip_wide[1:2, cols],
             y_s.at[:, cols], query_s, local,
         )
         own_state[:, cols] = state.astype(BF16)
@@ -458,7 +458,7 @@
 
     def sums_of(c, device):
         at, width = chunks[c]
-        return expand(all_sums[device], at // HEAD, width, 3)[0:1]
+        return sums_wide[pl.ds(device, 1), pl.ds(at, width)]
 
     upper = x.astype(F32)
     odd = z % 2
@@ -536,6 +536,7 @@
     rates_s[...] = jnp.zeros_like(rates_s)
     rates_s[0:1, 0 : rate_ref.shape[1]] = rate_ref[...]
     rates_s[1:2, 0 : rate_ref.shape[1]] = skip_ref[...]
+    skip_wide[...] = expand(rates_s[...], 0, inner, 3)
 
     last = len(chunks) - 1
     for step in range(last + 7):
@@ -561,6 +562,11 @@
                 if step - 4 - stage == 1 and stage == 0:
                     for by in range(1, nseq):
                         sum_copy(by).wait_recv()
+                    row = lax.broadcasted_iota(jnp.int32, (8, LANES), 0)
+                    packed = jnp.zeros((8, LANES), F32)
+                    for device in range(nseq):
+                        packed = jnp.where(row == device, all_sums[device], packed)
+                    sums_wide[...] = expand(packed, 0, inner, 3)
                 exchange(step - 4 - stage, stage)
         if 0 <= step - 2 <= last:
             forward(step - 2, 2)
@@ -630,6 +636,8 @@
             pltpu.SemaphoreType.DMA((chunks, 4)),
             pltpu.SemaphoreType.DMA((chunks,)),
             pltpu.VMEM((8, LANES), F32),
+            pltpu.VMEM((8, inner), F32),
+            pltpu.VMEM((8, inner), F32),
         ]
         + local_scratch(count),
         compiler_params=pltpu.CompilerParams(

time: 140 us -> 139 us (level)
  no operation moved by 1% of the time
where the time goes in v4:
time: 139 us
  Pallas kernels  133 us (96%)
  local copies, waits for them, and re-layouts  5.39 us (4%)
    pallas_call x1, Pallas kernels, fused(): pl.pallas_call(functools.partial(fused_kernel, nz, n, inner), out_shape=j...  133 us
    unnamed x2, local copies, waits for them, and re-layouts  4.52 us

profile of v4, /device:TPU:24, one launch (start us, length us, event | category | flops | bytes accessed | tf_op | source)
XLA Modules:
  0.0 138.8 jit_solution(12044875900201979240)
XLA Ops:
  0.7 1.4 copy.8
  2.0 0.9 pad.4.w_ref
  2.9 132.7 %fused.1 = bf16[512,2048]{1,0:T(8,128)(2,1)} custom-call(s32[1,11]{1,0:T(1,128)} %level_ref.1, s32[1]{0:T(128)S(6)} %sub.7.live_ref, bf16[512,4096]{1,0:T(8,128)(2,1)} %bitcast.6, bf16[128,2432]{1,0:T(8,128)(2,1)} %pad.4.w_ref, f32[4,2304]{1,0:T(4,128)} %conv_ref.1, f32[1,32]{1,0:T(1,128)} %bitcast.7, f32[1,32]{1,0:T(1,128)} %bitcast.8), custom_call_target="tpu_custom_call" | custom-call | tf_op jit(solution)/shard_map/fused/pallas_call | solution.py:608
  135.6 3.2 %copy.11 = bf16[1,512,2048]{2,1,0:T(8,128)(2,1)} copy(bf16[1,512,2048]{2,1,0:T(8,128)(2,1)} %bitcast.5) | data formatting | bytes 4194304
